TPU v7x, 128 devices: a whole 4x4x4 slice. The times are simulated.
128 devices in a mesh: rows: 16 (over z, x_lo, core), cols: 8 (over y, x_hi).
Axes of the slice: x: 4 (x_hi: 2, x_lo: 2; x = x_hi * 2 + x_lo), y: 4, z: 4, core: 2. Of those that a mesh axis runs over, the one named last changes fastest.
Arguments:
- fine_input: bfloat16 [2048, 2048, 64], P('rows', 'cols'), may hold values from -6 to 6
- cotangent: bfloat16 [2048, 2048, 64], P('rows', 'cols'), may hold values from -6 to 6
- lift_weight: bfloat16 [64, 256], replicated, may hold values from -3 to 3
- spectral_weight: bfloat16 [2, 512, 256, 256], P(None, ('rows', 'cols')), may hold values from -6 to 6
- skip_weight: bfloat16 [256, 256], replicated, may hold values from -0.375 to 0.375
- down_weight: bfloat16 [256, 64], replicated, may hold values from -0.375 to 0.375
- skip_fine: bfloat16 [64, 64], replicated, may hold values from -0.75 to 0.75
Outputs:
- grad_input: bfloat16 [2048, 2048, 64], P('rows', 'cols')
- grad_spectral: float32 [2, 512, 256, 256], P(None, ('rows', 'cols'))
- grad_lift: float32 [64, 256], replicated
- grad_skip: float32 [256, 256], replicated
- grad_down: float32 [256, 64], replicated
- grad_fine_skip: float32 [64, 64], replicated
All inputs are finite; a program needn't handle non-finite values.
Results may differ from a plain program's by a relative error of at most 0.018.
Values sent between devices are 32-bit elements; how exact they have to be, the bound alone decides.
No kernel may reach another device: no remote copies, remote signals or barrier semaphores. Data moves between devices by JAX's collectives and lax.ppermute only.
A program may use at most 128 MiB of HBM per device.

v0:
```python
import math

import jax
import jax.numpy as jnp
from jax import lax
from jax.sharding import PartitionSpec as P

ROW_MODES = 16
COL_MODES = 16


highest = lax.Precision.HIGHEST


def row_frequency():
    counter = jnp.arange(2 * ROW_MODES, dtype=jnp.int32)
    return jnp.where(counter < ROW_MODES, counter, counter - 2 * ROW_MODES)


def col_frequency():
    return jnp.arange(COL_MODES, dtype=jnp.int32)


def phase_table(frequency, start, count, period):
    position = start + jnp.arange(count, dtype=jnp.int32)
    phases = jnp.mod(frequency[:, None] * position[None, :], period)
    angles = phases.astype(jnp.float32) * (2.0 * math.pi / period)
    return (jnp.cos(angles), jnp.sin(angles))


def mode_weights(period_rows, period_cols):
    counter = jnp.arange(2 * ROW_MODES * COL_MODES, dtype=jnp.int32)
    doubled = jnp.where(jnp.mod(counter, COL_MODES) == 0, 1.0, 2.0).astype(jnp.float32)
    return doubled / float(period_rows * period_cols)


def analysis(grid_values, row_start, col_start, period_rows, period_cols):
    row_count, col_count, channels = grid_values.shape
    cos_rows, sin_rows = phase_table(row_frequency(), row_start, row_count, period_rows)
    cos_cols, sin_cols = phase_table(col_frequency(), col_start, col_count, period_cols)
    along_real = jnp.einsum("gm,nmi->ngi", cos_cols, grid_values, precision=highest)
    along_imag = -jnp.einsum("gm,nmi->ngi", sin_cols, grid_values, precision=highest)
    real_part = jnp.einsum("jn,ngi->jgi", cos_rows, along_real, precision=highest) + jnp.einsum(
        "jn,ngi->jgi", sin_rows, along_imag, precision=highest
    )
    imag_part = jnp.einsum("jn,ngi->jgi", cos_rows, along_imag, precision=highest) - jnp.einsum(
        "jn,ngi->jgi", sin_rows, along_real, precision=highest
    )
    return jnp.stack([real_part, imag_part]).reshape(2, 2 * ROW_MODES * COL_MODES, channels)


def synthesis(
    spectrum_real,
    spectrum_imag,
    row_start,
    col_start,
    row_count,
    col_count,
    period_rows,
    period_cols,
):
    channels = spectrum_real.shape[-1]
    real_grid = spectrum_real.reshape(2 * ROW_MODES, COL_MODES, channels)
    imag_grid = spectrum_imag.reshape(2 * ROW_MODES, COL_MODES, channels)
    cos_rows, sin_rows = phase_table(row_frequency(), row_start, row_count, period_rows)
    cos_cols, sin_cols = phase_table(col_frequency(), col_start, col_count, period_cols)
    turned_real = jnp.einsum("jn,jgo->ngo", cos_rows, real_grid, precision=highest) - jnp.einsum(
        "jn,jgo->ngo", sin_rows, imag_grid, precision=highest
    )
    turned_imag = jnp.einsum("jn,jgo->ngo", sin_rows, real_grid, precision=highest) + jnp.einsum(
        "jn,jgo->ngo", cos_rows, imag_grid, precision=highest
    )
    return jnp.einsum("gm,ngo->nmo", cos_cols, turned_real, precision=highest) - jnp.einsum(
        "gm,ngo->nmo", sin_cols, turned_imag, precision=highest
    )


def mix_modes(spectrum, kernel):
    kernel_real = kernel[0].astype(jnp.float32)
    kernel_imag = kernel[1].astype(jnp.float32)
    out_real = jnp.einsum("mi,mio->mo", spectrum[0], kernel_real, precision=highest) - jnp.einsum(
        "mi,mio->mo", spectrum[1], kernel_imag, precision=highest
    )
    out_imag = jnp.einsum("mi,mio->mo", spectrum[0], kernel_imag, precision=highest) + jnp.einsum(
        "mi,mio->mo", spectrum[1], kernel_real, precision=highest
    )
    return jnp.stack([out_real, out_imag])


def spectral_adjoint(spectrum, pulled, kernel):
    kernel_real = kernel[0].astype(jnp.float32)
    kernel_imag = kernel[1].astype(jnp.float32)
    grad_real = jnp.einsum("mi,mo->mio", spectrum[0], pulled[0], precision=highest) + jnp.einsum(
        "mi,mo->mio", spectrum[1], pulled[1], precision=highest
    )
    grad_imag = jnp.einsum("mi,mo->mio", spectrum[0], pulled[1], precision=highest) - jnp.einsum(
        "mi,mo->mio", spectrum[1], pulled[0], precision=highest
    )
    back_real = jnp.einsum("mio,mo->mi", kernel_real, pulled[0], precision=highest) + jnp.einsum(
        "mio,mo->mi", kernel_imag, pulled[1], precision=highest
    )
    back_imag = jnp.einsum("mio,mo->mi", kernel_real, pulled[1], precision=highest) - jnp.einsum(
        "mio,mo->mi", kernel_imag, pulled[0], precision=highest
    )
    return (jnp.stack([grad_real, grad_imag]), jnp.stack([back_real, back_imag]))


def block_sum(block):
    row_count, col_count, channels = block.shape
    return (
        block.astype(jnp.float32)
        .reshape(row_count // 4, 4, col_count // 4, 4, channels)
        .sum(axis=(1, 3))
    )


def expand(coarse_values):
    return jnp.repeat(jnp.repeat(coarse_values, 4, axis=0), 4, axis=1)


def lift_coarse(block, lift_weight):
    pooled = (block_sum(block) * (1.0 / 16.0)).astype(jnp.bfloat16)
    row_count, col_count, channels = pooled.shape
    coarse = jnp.dot(
        pooled.reshape(-1, channels), lift_weight, preferred_element_type=jnp.float32
    ).astype(jnp.bfloat16)
    return (pooled, coarse.reshape(row_count, col_count, -1))


def activation_pull(
    coarse,
    upstream,
    skip_weight,
    down_weight,
    mixed,
    weights,
    row_start,
    col_start,
    period_rows,
    period_cols,
):
    row_count, col_count, coarse_width = coarse.shape
    coarse_flat = coarse.reshape(-1, coarse_width)
    spectral = synthesis(
        weights[:, None] * mixed[0],
        weights[:, None] * mixed[1],
        row_start,
        col_start,
        row_count,
        col_count,
        period_rows,
        period_cols,
    )
    hidden_pre = spectral.reshape(-1, coarse_width) + jnp.dot(
        coarse_flat, skip_weight, preferred_element_type=jnp.float32
    )
    activated, pullback = jax.vjp(jax.nn.gelu, hidden_pre)
    summed = block_sum(upstream).astype(jnp.bfloat16)
    summed = summed.reshape(-1, summed.shape[-1])
    pulled_down = jnp.dot(summed, down_weight.T, preferred_element_type=jnp.float32)
    hidden_grad = pullback(pulled_down)[0].astype(jnp.bfloat16)
    return (activated.astype(jnp.bfloat16), summed, hidden_grad)


def reduce_modes(partial_modes):
    by_rows = lax.psum_scatter(partial_modes, "rows", scatter_dimension=1, tiled=True)
    return lax.psum_scatter(by_rows, "cols", scatter_dimension=1, tiled=True)


def spread_modes(owned_modes):
    by_cols = lax.all_gather(owned_modes, "cols", axis=1, tiled=True)
    return lax.all_gather(by_cols, "rows", axis=1, tiled=True)


def body(fine_input, cotangent, lift_weight, spectral_weight, skip_weight, down_weight, skip_fine):
    slab_rows, slab_cols, channels = fine_input.shape
    coarse_width = lift_weight.shape[1]
    local_rows = slab_rows // 4
    local_cols = slab_cols // 4
    total_rows = local_rows * lax.axis_size("rows")
    total_cols = local_cols * lax.axis_size("cols")
    period_rows = total_rows + total_rows // 8
    period_cols = total_cols + total_cols // 8
    row_start = lax.axis_index("rows") * local_rows
    col_start = lax.axis_index("cols") * local_cols
    weights = mode_weights(period_rows, period_cols)
    input_flat = fine_input.reshape(-1, channels)
    upstream_flat = cotangent.reshape(-1, channels)
    pooled, coarse = lift_coarse(fine_input, lift_weight)
    spectrum = reduce_modes(
        analysis(coarse.astype(jnp.float32), row_start, col_start, period_rows, period_cols)
    )
    mixed = spread_modes(mix_modes(spectrum, spectral_weight))
    activated, summed, hidden_grad = activation_pull(
        coarse,
        cotangent,
        skip_weight,
        down_weight,
        mixed,
        weights,
        row_start,
        col_start,
        period_rows,
        period_cols,
    )
    coarse_flat = coarse.reshape(-1, coarse_width)
    down_grad = jnp.dot(activated.T, summed, preferred_element_type=jnp.float32)
    skip_grad = jnp.dot(coarse_flat.T, hidden_grad, preferred_element_type=jnp.float32)
    pulled = (
        analysis(
            hidden_grad.astype(jnp.float32).reshape(local_rows, local_cols, coarse_width),
            row_start,
            col_start,
            period_rows,
            period_cols,
        )
        * weights[None, :, None]
    )
    pulled_owned = reduce_modes(pulled)
    grad_spectral, back_owned = spectral_adjoint(spectrum, pulled_owned, spectral_weight)
    back = spread_modes(back_owned)
    spectral_back = synthesis(
        back[0], back[1], row_start, col_start, local_rows, local_cols, period_rows, period_cols
    )
    coarse_grad = (
        spectral_back.reshape(-1, coarse_width)
        + jnp.dot(hidden_grad, skip_weight.T, preferred_element_type=jnp.float32)
    ).astype(jnp.bfloat16)
    lift_grad = jnp.dot(
        pooled.reshape(-1, channels).T, coarse_grad, preferred_element_type=jnp.float32
    )
    pooled_grad = jnp.dot(coarse_grad, lift_weight.T, preferred_element_type=jnp.float32).reshape(
        local_rows, local_cols, channels
    )
    fine_term = jnp.dot(upstream_flat, skip_fine.T, preferred_element_type=jnp.float32)
    fine_grad = jnp.dot(input_flat.T, upstream_flat, preferred_element_type=jnp.float32)
    grad_input = (
        fine_term.reshape(slab_rows, slab_cols, channels) + expand(pooled_grad) * (1.0 / 16.0)
    ).astype(jnp.bfloat16)
    totals = lax.psum((lift_grad, skip_grad, down_grad, fine_grad), ("rows", "cols"))
    coarse_scale = 1.0 / math.sqrt(total_rows * total_cols)
    fine_scale = 1.0 / math.sqrt(16 * total_rows * total_cols)
    return (
        grad_input,
        grad_spectral,
        totals[0] * coarse_scale,
        totals[1] * coarse_scale,
        totals[2] * coarse_scale,
        totals[3] * fine_scale,
    )


def solution(mesh):
    return jax.shard_map(
        body,
        mesh=mesh,
        in_specs=(
            P("rows", "cols", None),
            P("rows", "cols", None),
            P(),
            P(None, ("rows", "cols"), None, None),
            P(),
            P(),
            P(),
        ),
        out_specs=(
            P("rows", "cols", None),
            P(None, ("rows", "cols"), None, None),
            P(),
            P(),
            P(),
            P(),
        ),
        check_vma=False,
    )
```

profile of v0, /device:TPU:1, one launch (start us, length us, event | category | flops | bytes accessed | tf_op | source)
XLA Modules:
  0.0 712.1 jit_solution(3771695612683221369)
XLA Ops:
  7.2 8.4 %copy.105 = bf16[128,256,64]{2,1,0:T(8,128)(2,1)} copy(bf16[128,256,64]{1,2,0:T(8,128)(2,1)} %param.7) | data formatting | bytes 8388608 | tf_op args[0]
  15.7 9.4 %convert_reduce_fusion = f32[32,64,64]{2,1,0:T(8,128)S(1)} fusion(bf16[32,4,64,4,64]{4,3,2,1,0:T(4,128)(2,1)} %bitcast.179), kind=kLoop, calls=%fused_computation | loop fusion | flops 4063232 | bytes 4718592 | tf_op jit(solution)/shard_map/reduce_sum | solution.py:113
  33.9 61.1 %reduce-scatter.5.cloned.1.call-done = f32[2,32,256]{2,1,0:T(8,128)} async-done(((f32[2,512,256]{2,1,0:T(8,128)}), f32[2,32,256]{2,1,0:T(8,128)}) %reduce-scatter.5.cloned.1.call-update) | async-done | bytes 65552 | tf_op jit(solution)/shard_map/reduce_scatter | solution.py:166
  96.3 81.5 %all-reduce.7.cloned.1.call-done = f32[2,32,256]{2,1,0:T(8,128)} async-done(((f32[2,32,256]{2,1,0:T(8,128)}), f32[2,32,256]{2,1,0:T(8,128)}) %all-reduce.7.cloned.1.call-update) | async-done | bytes 65552
  179.9 27.9 %all_gather.12 = f32[2,32,256]{2,0,1:T(2,128)S(1)} all-gather(f32[2,4,256]{2,0,1:T(2,128)S(1)} %pad_maximum_fusion.2), channel_id=1, replica_groups=mesh['rows'=16,'cols'=8] {'cols'}, dimensions={1}, use_global_device_ids=true | all-gather | bytes 73728 | tf_op jit(solution)/shard_map/all_gather | solution.py:171
  208.4 8.4 %copy.104 = bf16[128,256,64]{2,1,0:T(8,128)(2,1)} copy(bf16[128,256,64]{1,2,0:T(8,128)(2,1)} %param.8) | data formatting | bytes 8388608 | tf_op args[1]
  216.9 10.3 %reduce = bf16[32,64,64]{2,1,0:T(8,128)(2,1)} reduce(bf16[32,4,64,4,64]{4,3,2,1,0:T(4,128)(2,1)} %bitcast.180, bf16[]{:T(256)} %constant.106), dimensions={1,3}, to_apply=%region_0.1.clone | reduce | flops 1966080 | bytes 4456450 | tf_op jit(solution)/shard_map/reduce_sum | solution.py:113
  227.2 23.6 %all-gather.3.cloned.1.call-done = f32[2,512,256]{2,1,0:T(8,128)} async-done(((f32[2,32,256]{2,1,0:T(8,128)}), f32[2,512,256]{2,1,0:T(8,128)}) %all-gather.3.cloned.1.call-update) | async-done | bytes 1048592 | tf_op jit(solution)/shard_map/all_gather | solution.py:172
  250.8 1.3 fusion.317
  256.2 2.1 fusion.31
  258.4 1.9 convolution_subtract_fusion.1
  261.4 1.5 fusion.7
  270.0 57.6 %reduce-scatter.7.cloned.1.call-done = f32[2,32,256]{2,1,0:T(8,128)} async-done(((f32[2,512,256]{2,1,0:T(8,128)}), f32[2,32,256]{2,1,0:T(8,128)}) %reduce-scatter.7.cloned.1.call-update) | async-done | bytes 65552 | tf_op jit(solution)/shard_map/reduce_scatter | solution.py:166
  327.7 82.3 %all-reduce.9.cloned.1.call-done = f32[2,32,256]{2,1,0:T(8,128)} async-done(((f32[2,32,256]{2,1,0:T(8,128)}), f32[2,32,256]{2,1,0:T(8,128)}) %all-reduce.9.cloned.1.call-update) | async-done | bytes 65552
  412.9 27.9 %all_gather.14 = f32[2,32,256]{2,0,1:T(2,128)S(1)} all-gather(f32[2,4,256]{2,0,1:T(2,128)S(1)} %pad_maximum_fusion.3), channel_id=1, replica_groups=mesh['rows'=16,'cols'=8] {'cols'}, dimensions={1}, use_global_device_ids=true | all-gather | bytes 73728 | tf_op jit(solution)/shard_map/all_gather | solution.py:171
  441.5 4.7 convolution_bitcast_fusion.2
  446.2 74.6 %psum.31 = f32[64,64]{1,0:T(8,128)S(1)} all-reduce(f32[64,64]{1,0:T(8,128)S(1)} %convolution_bitcast_fusion.2), channel_id=1, replica_groups=mesh['rows'=16,'cols'=8] {'rows','cols'}, use_global_device_ids=true, to_apply=%region_9.10 | all-reduce | flops 4096 | bytes 32768 | tf_op jit(solution)/shard_map/psum | solution.py:240
  521.5 1.2 fusion.319
  522.6 1.5 fusion.10
  524.5 1.5 pad_maximum_fusion
  525.9 1.3 fusion.316
  531.2 1.9 fusion.28
  533.2 1.9 convolution_subtract_fusion
  537.9 2.5 broadcast_in_dim.20
  540.4 4.0 copy.141
  544.4 4.3 broadcast_in_dim.21
  548.7 9.3 %copy.142 = f32[128,256,64]{1,2,0:T(8,128)} copy(f32[128,256,64]{0,2,1:T(8,128)} %bitcast.178) | data formatting | bytes 16777216 | tf_op jit(solution)/shard_map/mul | solution.py:238
  558.0 7.9 %add_convert_fusion = bf16[128,256,64]{1,2,0:T(8,128)(2,1)} fusion(f32[128,256,64]{1,2,0:T(8,128)} %copy.142, bf16[128,256,64]{1,2,0:T(8,128)(2,1)} %param.8, bf16[64,64]{1,0:T(8,128)(2,1)S(1)} %copy-done.9), kind=kOutput, calls=%fused_computation.1 | convolution fusion | flops 272629760 | bytes 16785408 | tf_op jit(solution)/shard_map/dot_general | solution.py:235
  565.9 134.2 %all-reduce.11.cloned.1.call-done = (f32[64,256]{1,0:T(8,128)}, f32[256,256]{1,0:T(8,128)}, f32[256,64]{0,1:T(8,128)}) async-done(((f32[64,256]{1,0:T(8,128)}, f32[256,256]{1,0:T(8,128)}, f32[256,64]{0,1:T(8,128)}), (f32[64,256]{1,0:T(8,128)}, f32[256,256]{1,0:T(8,128)}, f32[256,64]{0,1:T(8,128)})) %all-reduce.11.cloned.1.call-update) | async-done | bytes 393232 | tf_op jit(solution)/shard_map/psum | solution.py:240
  700.2 1.7 broadcast_multiply_fusion.2
  701.9 1.5 broadcast_multiply_fusion.3
  703.3 1.5 broadcast_multiply_fusion.4
  (102 shorter events, 35.5 us)
Async XLA Ops:
  7.2 253.2 %copy-start = (bf16[256,256]{1,0:T(8,128)(2,1)S(1)}, bf16[256,256]{1,0:T(8,128)(2,1)}, u32[]{:S(2)}) copy-start(bf16[256,256]{1,0:T(8,128)(2,1)} %param.11) | copy-start | bytes 393220
  7.2 87.8 %reduce-scatter.5.cloned.1.call-start = ((), (), s32[]{:S(2)}) async-start(), calls=%async_computation.2 | async-start | bytes 1114112 | tf_op jit(solution)/shard_map/reduce_scatter | solution.py:166
  15.7 10.4 %copy-start.8 = (bf16[64,256]{1,0:T(8,128)(2,1)S(1)}, bf16[64,256]{1,0:T(8,128)(2,1)}, u32[]{:S(2)}) copy-start(bf16[64,256]{1,0:T(8,128)(2,1)} %param.9) | copy-start | bytes 98308
  25.2 0.8 copy-start.2
  32.1 63.0 %copy-start.11 = (u32[128]{0:T(128)S(1)}, u32[128]{0:T(128)}, u32[]{:S(2)}) copy-start(u32[128]{0:T(128)} %constant.109) | copy-start | bytes 1540
  32.1 146.5 %copy-start.1 = (bf16[2,4,256,256]{3,2,1,0:T(8,128)(2,1)S(1)}, bf16[2,4,256,256]{3,2,1,0:T(8,128)(2,1)}, u32[]{:S(2)}) copy-start(bf16[2,4,256,256]{3,2,1,0:T(8,128)(2,1)} %param.10) | copy-start | bytes 3145732
  33.8 144.0 %all-reduce.7.cloned.1.call-start = ((), (), s32[]{:S(2)}) async-start(), calls=%async_computation.6 | async-start | bytes 131072
  95.0 155.8 %all-gather.3.cloned.1.call-start = ((), (), s32[]{:S(2)}) async-start(), calls=%async_computation.3 | async-start | bytes 1114112 | tf_op jit(solution)/shard_map/all_gather | solution.py:172
  208.4 119.2 %reduce-scatter.7.cloned.1.call-start = ((), (), s32[]{:S(2)}) async-start(), calls=%async_computation.4 | async-start | bytes 1114112 | tf_op jit(solution)/shard_map/reduce_scatter | solution.py:166
  260.3 1.0 copy-start.6
  260.3 1.0 copy-start.10
  260.8 2.1 copy-start.4
  269.9 140.1 %all-reduce.9.cloned.1.call-start = ((), (), s32[]{:S(2)}) async-start(), calls=%async_computation.7 | async-start | bytes 131072
  327.6 198.3 %all-gather.5.cloned.1.call-start = ((), (), s32[]{:S(2)}) async-start(), calls=%async_computation.5 | async-start | bytes 1114112 | tf_op jit(solution)/shard_map/all_gather | solution.py:172
  441.4 258.8 %all-reduce.11.cloned.1.call-start = ((), (), s32[]{:S(2)}) async-start(), calls=%async_computation.8 | async-start | bytes 786432 | tf_op jit(solution)/shard_map/psum | solution.py:240
  441.5 81.2 %copy-start.7 = (bf16[32,64,64]{2,1,0:T(8,128)(2,1)S(1)}, bf16[32,64,64]{2,1,0:T(8,128)(2,1)}, u32[]{:S(2)}) copy-start(bf16[32,64,64]{2,1,0:T(8,128)(2,1)} %reduce) | copy-start | bytes 786436
  520.8 1.8 copy-start.5
  535.1 1.0 copy-start.3
  548.7 9.3 %copy-start.9 = (bf16[64,64]{1,0:T(8,128)(2,1)S(1)}, bf16[64,64]{1,0:T(8,128)(2,1)}, u32[]{:S(2)}) copy-start(bf16[64,64]{1,0:T(8,128)(2,1)} %param.13) | copy-start | bytes 24580
Sparse Core Ops, SparseCore 0:
  33.9 60.9 reduce-scatter.4
  97.6 80.1 all-reduce.6
  208.5 42.2 all-gather.2
  270.1 57.5 reduce-scatter.6
  330.1 79.9 all-reduce.8
  441.5 42.3 all-gather.4
  558.1 141.9 all-reduce.10
where the time goes:
time: 722 us; the launch traced here: 712 us
  waiting for transfers between devices  441 us (61%)
  blocking collectives  130 us (18%)
  matrix products  49.2 us (7%)
  local copies, waits for them, and re-layouts  46.7 us (6%)
  other arithmetic  29.2 us (4%)
  between operations  15.7 us (2%)
    unnamed x9, waiting for transfers between devices  164 us
    psum x1, waiting for transfers between devices, body(): lax.psum((lift_grad, skip_grad, down_grad, fine_grad), ('rows', 'cols'))  134 us
    reduce_scatter x2, waiting for transfers between devices, reduce_modes(): lax.psum_scatter(partial_modes, 'rows', scatter_dimension=1, tiled=True)  119 us
    psum x1, blocking collectives, body(): lax.psum((lift_grad, skip_grad, down_grad, fine_grad), ('rows', 'cols'))  74.6 us
    all_gather x2, blocking collectives, spread_modes(): by_cols = lax.all_gather(owned_modes, 'cols', axis=1, tiled=True)  55.7 us
    all_gather x2, waiting for transfers between devices, spread_modes(): return lax.all_gather(by_cols, 'rows', axis=1, tiled=True)  23.6 us
    reduce_sum x2, other arithmetic, block_sum(): return block.astype(jnp.float32).reshape(row_count // 4, 4, col_count //...  19.7 us
    unnamed x27, local copies, waits for them, and re-layouts  19.4 us
  transfers between devices with their start and end apart: 7, of which 6 were waited for; matrix products, arithmetic and copies ran while one was open for 5% of the time, Pallas kernels for 0%

commit v1 on v0

v1 whole, which is shorter than its diff:
```python
import math

import jax
import jax.numpy as jnp
import numpy as np
from jax import lax
from jax.experimental import pallas as pl
from jax.experimental.pallas import tpu as pltpu
from jax.sharding import Mesh, PartitionSpec as P

F32 = jnp.float32
BF16 = jnp.bfloat16
HIGH = lax.Precision.HIGHEST

ROWS = ("z", "xl", "core")
COLS = ("y", "xh")
ALL = ROWS + COLS
SAME_CORE = ("z", "xl", "y", "xh")

PERIOD = 576
N_R, N_C = 16, 8
LR, LC = 32, 64
VMEM = 20 * 1024 * 1024


def _split(table):
    high = table.astype(BF16)
    low = (table - high.astype(np.float64)).astype(BF16)
    return high, low


def _row_tables():
    j = np.arange(32)
    f = np.where(j < 16, j, j - 32)
    n = np.arange(N_R * LR)
    angle = 2.0 * np.pi * np.mod(f[:, None] * n[None, :], PERIOD) / PERIOD
    cos = np.cos(angle).reshape(32, N_R, LR)
    sin = np.sin(angle).reshape(32, N_R, LR)
    m = np.stack([np.stack([cos, sin], -1), np.stack([-sin, cos], -1)], 0)
    m = m.transpose(2, 1, 0, 3, 4)
    full = np.einsum("rjpnq,ts->rjptnqs", m, np.eye(4))
    natural = full.transpose(0, 2, 1, 3, 4, 5, 6).reshape(N_R, 256, 256)
    split = full.reshape(N_R, 8, 2, 2, 2, 4, 256)
    split = split.transpose(0, 2, 1, 3, 4, 5, 6)
    by_core = np.stack([split[r, [r & 1, 1 - (r & 1)]] for r in range(N_R)])
    by_core = by_core.reshape(N_R, 256, 256)
    return tuple(
        np.concatenate(_split(a), -1) for a in (natural, by_core.transpose(0, 2, 1), by_core)
    )


def _col_tables():
    g = np.arange(16)
    m = np.arange(N_C * LC)
    angle = 2.0 * np.pi * np.mod(g[:, None] * m[None, :], PERIOD) / PERIOD
    both = np.stack([np.cos(angle), -np.sin(angle)], 0).reshape(2, 4, 4, N_C, LC)
    table = both.transpose(3, 1, 0, 2, 4).reshape(N_C, 32, LC)
    high, low = _split(table)
    down = np.concatenate([high, low], 1)
    up = np.concatenate([high, low, high], 1).transpose(0, 2, 1)
    wide_high, wide_low = (np.repeat(a, 4, axis=2) for a in _split(table / 16.0))
    spread = np.repeat(np.eye(LC), 4, axis=1) / 16.0
    spread = np.broadcast_to(spread.astype(BF16), (N_C, LC, 4 * LC))
    fine = np.concatenate([wide_high, wide_low, wide_high, spread], 1)
    return down, up, fine


def _dot(a, b, contract=((1,), (0,)), precision=None):
    return lax.dot_general(a, b, (contract, ((), ())), precision=precision, preferred_element_type=F32)


def _dot_nt(a, b, precision=None):
    return _dot(a, b, ((1,), (1,)), precision)


def _halves(a):
    high = a.astype(BF16)
    return high, (a - high.astype(F32)).astype(BF16)


def _turn(table, data):
    high, low = _halves(data)
    return _dot(table, jnp.concatenate([high, high], 0)) + _dot(table[:, :256], low)


def _mode_weight(place_ref):
    row = lax.broadcasted_iota(jnp.int32, (8, 256), 0)
    first = jnp.logical_and(lax.rem(row, 4) == 0, lax.rem(place_ref[1], 4) == 0)
    return jnp.where(first, 1.0, 2.0) * (1.0 / (PERIOD * PERIOD))


def _pool_matrix():
    row = lax.broadcasted_iota(jnp.int32, (512, 64), 0)
    col = lax.broadcasted_iota(jnp.int32, (512, 64), 1)
    return jnp.where(lax.rem(row, 256) // 4 == col, 1.0, 0.0).astype(BF16)


def _sum_blocks(ref, i, pool):
    rows = ref[pl.ds(i * 16, 16)].astype(F32).reshape(4, 4, 64, 256).sum(1).reshape(256, 256)
    return _dot(jnp.concatenate(_halves(rows), 1), pool)


def _pool_kernel(
    place_ref, x_any, natural_any, down_any, up_any, wide_any, syn_any, ana_any,
    p_ref, ps_ref, pst_ref, down_ref, up_ref, wide_ref, syn_ref, ana_ref, x_ref,
    rows_ref, c_ref, x_sem, sem,
):
    r, c = place_ref[0], place_ref[1]
    first = pltpu.make_async_copy(down_any.at[c], down_ref, sem.at[0])
    first.start()
    chunks = [
        pltpu.make_async_copy(x_any.at[pl.ds(32 * k, 32)], x_ref.at[pl.ds(32 * k, 32)], x_sem.at[k])
        for k in range(4)
    ]
    for chunk in chunks:
        chunk.start()
    rest = [
        pltpu.make_async_copy(source.at[at], target, sem.at[k + 1])
        for k, (source, at, target) in enumerate(
            [
                (natural_any, r, rows_ref),
                (up_any, c, up_ref),
                (wide_any, c, wide_ref),
                (syn_any, r, syn_ref),
                (ana_any, r, ana_ref),
            ]
        )
    ]
    for copy in rest:
        copy.start()
    pool = _pool_matrix()
    first.wait()
    down = down_ref[...]
    def narrow(i, xp):
        for n in range(4):
            wide = jnp.concatenate([xp[n], xp[n]], 0).astype(F32).T.astype(BF16)
            ps_ref[i * 4 + n] = wide
            modes = _dot(down, wide)
            modes = modes[:32] + modes[32:]
            at = (i * 4 + n) * 8
            for g in range(4):
                c_ref[g, at : at + 8, :] = modes[g * 8 : (g + 1) * 8]

    held = None
    for i in range(8):
        if i % 2 == 0:
            chunks[i // 2].wait()
        xp = (_sum_blocks(x_ref, i, pool) * (1.0 / 16.0)).astype(BF16)
        xp = [xp[64 * n : 64 * n + 64] for n in range(4)]
        pst_ref[:, 256 * i : 256 * (i + 1)] = jnp.concatenate(xp, 1)
        if held is not None:
            narrow(i - 1, held)
        held = xp
    narrow(7, held)
    for copy in rest:
        copy.wait()
    first_half = lax.broadcasted_iota(jnp.int32, (128, 128), 1) < 64
    for g in range(4):
        done = _turn(rows_ref[...], c_ref[g])
        done = jnp.where(first_half, done[:128], done[128:])
        p_ref[:, g] = done.reshape(32, 4, 128)


def pool_call(place, *operands):
    vm = pl.BlockSpec(memory_space=pltpu.VMEM)
    operands = [pltpu.with_memory_space_constraint(jnp.asarray(a), pltpu.HBM) for a in operands]
    return pl.pallas_call(
        _pool_kernel,
        in_specs=[pl.BlockSpec(memory_space=pltpu.SMEM)] + [pl.BlockSpec(memory_space=pltpu.HBM)] * 7,
        out_specs=[vm] * 9,
        out_shape=[
            jax.ShapeDtypeStruct((32, 4, 4, 128), F32),
            jax.ShapeDtypeStruct((32, 64, 128), BF16),
            jax.ShapeDtypeStruct((64, 2048), BF16),
            jax.ShapeDtypeStruct((64, 64), BF16),
            jax.ShapeDtypeStruct((64, 96), BF16),
            jax.ShapeDtypeStruct((160, 256), BF16),
            jax.ShapeDtypeStruct((256, 512), BF16),
            jax.ShapeDtypeStruct((256, 512), BF16),
            jax.ShapeDtypeStruct((128, 64, 256), BF16),
        ],
        scratch_shapes=[
            pltpu.VMEM((256, 512), BF16),
            pltpu.VMEM((4, 256, 128), F32),
            pltpu.SemaphoreType.DMA((4,)),
            pltpu.SemaphoreType.DMA((6,)),
        ],
        compiler_params=pltpu.CompilerParams(vmem_limit_bytes=VMEM),
        name="pool",
    )(place, *operands)


def _upstream_kernel(x_ref, u_ref, su_ref, sut_ref, fine_ref):
    pool = _pool_matrix()
    term = jnp.zeros((64, 64), F32)
    for i in range(8):
        us = _sum_blocks(u_ref, i, pool).astype(BF16)
        us = [us[64 * n : 64 * n + 64] for n in range(4)]
        sut_ref[:, 256 * i : 256 * (i + 1)] = jnp.concatenate(us, 1)
        for n in range(4):
            su_ref[i * 4 + n] = us[n].astype(F32).T.astype(BF16)
        x_all = jnp.concatenate([x_ref[i * 16 + a] for a in range(16)], 1)
        u_all = jnp.concatenate([u_ref[i * 16 + a] for a in range(16)], 1)
        term += _dot_nt(x_all, u_all)
    fine_ref[...] = term


def upstream_call(x, u):
    vm = pl.BlockSpec(memory_space=pltpu.VMEM)
    return pl.pallas_call(
        _upstream_kernel,
        in_specs=[vm] * 2,
        out_specs=[vm] * 3,
        out_shape=[
            jax.ShapeDtypeStruct((32, 64, 64), BF16),
            jax.ShapeDtypeStruct((64, 2048), BF16),
            jax.ShapeDtypeStruct((64, 64), F32),
        ],
        compiler_params=pltpu.CompilerParams(vmem_limit_bytes=VMEM),
        name="upstream",
    )(x, u)


def _mix_kernel(place_ref, got_ref, lift_ref, w_ref, mixed_ref, p_ref, s_ref):
    p = got_ref[...].sum(0)
    p = jnp.concatenate([p[:, :64], p[:, 64:]], 0)
    p_ref[...] = p
    s = _dot(jnp.concatenate(_halves(p), 0), lift_ref[...])
    s = s[:8] + s[8:]
    s_ref[...] = s
    parts = jnp.concatenate(_halves(s), 0)
    row = lax.broadcasted_iota(jnp.int32, (8, 256), 0)
    sign = jnp.where(row < 4, -1.0, 1.0)
    total = jnp.zeros((8, 256), F32)
    for t in range(4):
        a = _dot(parts, w_ref[0, t])
        b = _dot(parts, w_ref[1, t])
        a = a[:8] + a[8:]
        b = b[:8] + b[8:]
        b = jnp.concatenate([b[4:], b[:4]], 0)
        total = jnp.where(lax.rem(row, 4) == t, a + sign * b, total)
    mixed_ref[...] = jnp.broadcast_to((total * _mode_weight(place_ref))[None], (64, 8, 256))


def mix_call(place, got, lift, weight):
    vm = pl.BlockSpec(memory_space=pltpu.VMEM)
    return pl.pallas_call(
        _mix_kernel,
        in_specs=[pl.BlockSpec(memory_space=pltpu.SMEM), vm, vm, vm],
        out_specs=[vm] * 3,
        out_shape=[
            jax.ShapeDtypeStruct((64, 8, 256), F32),
            jax.ShapeDtypeStruct((8, 64), F32),
            jax.ShapeDtypeStruct((8, 256), F32),
        ],
        compiler_params=pltpu.CompilerParams(vmem_limit_bytes=VMEM),
        name="mix",
    )(place, got, lift, weight)


def _hidden_kernel(
    place_ref, mine_ref, other_ref, ps_ref, pst_ref, su_ref, sut_ref, lift_ref, skip_ref, downt_ref, fine_ref,
    syn_ref, ana_ref, up_ref, down_ref, keep_ref, send_ref, hl_ref, t_ref, c_ref, q_ref, d_ref,
):
    for g in range(4):
        modes = jnp.concatenate([mine_ref[:, g].reshape(128, 256), other_ref[:, g].reshape(128, 256)], 0)
        turned = _turn(syn_ref[...], modes)
        t_ref[:, g * 8 : (g + 1) * 8, :] = turned.reshape(32, 8, 256)
    both = _dot(lift_ref[...], skip_ref[...])
    high, low = _halves(both)
    right = jnp.concatenate([high, low], 0)
    downt = downt_ref[...]
    q_ref[...] = jnp.zeros((64, 256), F32)
    d_ref[...] = jnp.zeros((64, 256), F32)
    root = math.sqrt(2.0 / math.pi)

    def group(i, carry):
        first = _dot(ps_ref[pl.ds(i * 4, 4)].reshape(256, 128), right)
        pulled = _dot(su_ref[pl.ds(i * 4, 4)].reshape(256, 64), downt)
        field = []
        for n in range(4):
            th, tl = _halves(t_ref[i * 4 + n])
            field.append(_dot(up_ref[...], jnp.concatenate([th, th, tl], 0)))
        v = first + jnp.concatenate(field, 0)
        v2 = v * v
        half = 0.5 + 0.5 * jnp.tanh(v * (root + (root * 0.044715) * v2))
        act = (v * half).astype(BF16)
        slope = half * (1.0 + v * (2.0 * root + (6.0 * root * 0.044715) * v2) * (1.0 - half))
        hg = (pulled * slope).astype(BF16)
        lanes = pl.ds(pl.multiple_of(i * 256, 256), 256)
        q_ref[...] += _dot(pst_ref[:, lanes], hg)
        d_ref[...] += _dot(sut_ref[:, lanes], act)
        for n in range(4):
            modes = _dot(down_ref[...], hg[n * 64 : (n + 1) * 64])
            modes = modes[:32] + modes[32:]
            at = pl.multiple_of((i * 4 + n) * 8, 8)
            for g in range(4):
                c_ref[g, pl.ds(at, 8), :] = modes[g * 8 : (g + 1) * 8]
        hl_ref[:, lanes] = _dot_nt(high, hg).astype(BF16)
        return carry

    lax.fori_loop(0, 8, group, 0, unroll=8)
    for g in range(4):
        done = _turn(ana_ref[...], c_ref[g])
        keep_ref[:, g, :, 0:256] = done[:128].reshape(16, 8, 256)
        send_ref[:, g, :, 0:256] = done[128:].reshape(16, 8, 256)
    core = place_ref[2]
    blank = jnp.zeros((64, 64), F32)

    def extras(ref, low_half):
        ref[:, :, :, 256:384] = jnp.zeros((16, 4, 8, 128), F32)
        q = jnp.where(low_half, q_ref[:, 0:128], q_ref[:, 128:256])
        d = jnp.where(low_half, d_ref[:, 0:128], d_ref[:, 128:256])
        planes = [q[:, :64], q[:, 64:], d[:, :64], d[:, 64:], fine_ref[...]]
        for k, plane in enumerate(planes):
            ref[:, :, k, 256:384] = jnp.concatenate([blank, plane], 1).reshape(16, 4, 128)

    extras(keep_ref, core == 0)
    extras(send_ref, core == 1)


def hidden_call(place, *operands):
    vm = pl.BlockSpec(memory_space=pltpu.VMEM)
    return pl.pallas_call(
        _hidden_kernel,
        in_specs=[pl.BlockSpec(memory_space=pltpu.SMEM)] + [vm] * 14,
        out_specs=[vm] * 3,
        out_shape=[
            jax.ShapeDtypeStruct((16, 4, 8, 384), F32),
            jax.ShapeDtypeStruct((16, 4, 8, 384), F32),
            jax.ShapeDtypeStruct((64, 2048), BF16),
        ],
        scratch_shapes=[
            pltpu.VMEM((32, 32, 256), F32),
            pltpu.VMEM((4, 256, 256), F32),
            pltpu.VMEM((64, 256), F32),
            pltpu.VMEM((64, 256), F32),
        ],
        compiler_params=pltpu.CompilerParams(vmem_limit_bytes=VMEM),
        name="hidden",
    )(place, *operands)


def _adjoint_kernel(place_ref, got_ref, p_ref, w_ref, pulled_ref, block_ref):
    total = got_ref[...].sum(0)
    pulled = total[:, :256] * _mode_weight(place_ref)
    pulled_ref[...] = pulled
    parts = jnp.concatenate(_halves(pulled), 0)
    row = lax.broadcasted_iota(jnp.int32, (8, 256), 0)
    sign = jnp.where(row < 4, 1.0, -1.0)
    back = jnp.zeros((8, 256), F32)
    for t in range(4):
        a = _dot_nt(parts, w_ref[0, t])
        b = _dot_nt(parts, w_ref[1, t])
        a = a[:8] + a[8:]
        b = b[:8] + b[8:]
        b = jnp.concatenate([b[4:], b[:4]], 0)
        back = jnp.where(lax.rem(row, 4) == t, a + sign * b, back)
    block = jnp.concatenate([back, p_ref[...], total[:, 320:384]], 1)
    block_ref[...] = jnp.broadcast_to(block[None], (64, 8, 384))


def adjoint_call(place, got, p, weight):
    vm = pl.BlockSpec(memory_space=pltpu.VMEM)
    return pl.pallas_call(
        _adjoint_kernel,
        in_specs=[pl.BlockSpec(memory_space=pltpu.SMEM)] + [vm] * 3,
        out_specs=[vm] * 2,
        out_shape=[
            jax.ShapeDtypeStruct((8, 256), F32),
            jax.ShapeDtypeStruct((64, 8, 384), F32),
        ],
        compiler_params=pltpu.CompilerParams(vmem_limit_bytes=VMEM),
        name="adjoint",
    )(place, got, p, weight)


def _gathered(ref, lift):
    high, low = _halves(ref[:, :, :, 0:256].reshape(512, 256))
    narrow = _dot_nt(high, lift) + _dot_nt(low, lift)
    p_high, p_low = _halves(ref[:, :, :, 256:384].reshape(512, 128).T[:64])
    both = _dot(jnp.concatenate([p_high, p_low], 0), high)
    return narrow, both[:64] + both[64:] + _dot(p_high, low)


def _outer_kernel(s_ref, pulled_ref, mine_ref, lift_ref, grad_any, narrow_ref, sum_ref, grad_ref, sem):
    s = s_ref[...].T
    pulled = pulled_ref[...]
    copies = []
    for t in range(4):
        s0, s1 = s[:, t : t + 1], s[:, 4 + t : 5 + t]
        p0, p1 = pulled[t : t + 1], pulled[4 + t : 5 + t]
        grad_ref[0, t] = s0 * p0 + s1 * p1
        grad_ref[1, t] = s0 * p1 - s1 * p0
        for part in range(2):
            copies.append(pltpu.make_async_copy(grad_ref.at[part, t], grad_any.at[part, t], sem.at[part, t]))
            copies[-1].start()
    narrow_ref[...], sum_ref[...] = _gathered(mine_ref, lift_ref[...])
    for copy in copies:
        copy.wait()


def outer_call(s, pulled, mine, lift):
    vm = pl.BlockSpec(memory_space=pltpu.VMEM)
    return pl.pallas_call(
        _outer_kernel,
        in_specs=[vm] * 4,
        out_specs=[pl.BlockSpec(memory_space=pl.ANY), vm, vm],
        out_shape=[
            jax.ShapeDtypeStruct((2, 4, 256, 256), F32),
            jax.ShapeDtypeStruct((512, 64), F32),
            jax.ShapeDtypeStruct((64, 256), F32),
        ],
        scratch_shapes=[pltpu.VMEM((2, 4, 256, 256), F32), pltpu.SemaphoreType.DMA((2, 4))],
        compiler_params=pltpu.CompilerParams(vmem_limit_bytes=VMEM),
        cost_estimate=pl.CostEstimate(flops=2_000_000, bytes_accessed=2_200_000, transcendentals=0),
        name="outer",
    )(s, pulled, mine, lift)


def _term_kernel(u_ref, sf_ref, out_ref):
    row = lax.broadcasted_iota(jnp.int32, (256, 256), 0)
    col = lax.broadcasted_iota(jnp.int32, (256, 256), 1)
    sf = sf_ref[...].astype(F32)
    sf = jnp.concatenate([jnp.concatenate([sf] * 4, 1)] * 4, 0)
    sf = jnp.where(row // 64 == col // 64, sf, 0.0).astype(BF16)
    for n in range(32):
        out_ref[4 * n : 4 * n + 4] = _dot(sf, u_ref[4 * n : 4 * n + 4].reshape(256, 256)).reshape(4, 64, 256)


def term_call(u, sf):
    vm = pl.BlockSpec(memory_space=pltpu.VMEM)
    return pl.pallas_call(
        _term_kernel,
        in_specs=[vm] * 2,
        out_specs=vm,
        out_shape=jax.ShapeDtypeStruct((128, 64, 256), F32),
        compiler_params=pltpu.CompilerParams(vmem_limit_bytes=VMEM),
        cost_estimate=pl.CostEstimate(flops=400_000_000, bytes_accessed=12_000_000, transcendentals=0),
        name="term",
    )(u, sf)


def _fine_kernel(
    place_ref, term_ref, hl_ref, mine_ref, narrow_ref, sum_ref, other_ref, lift_ref, skip_ref, syn_ref, wide_ref,
    out_any, lift_out, skip_out, down_out, fine_out, t_ref, out_ref, sem,
):
    lift = lift_ref[...]
    far_narrow, far_sum = _gathered(other_ref, lift)
    narrow = [a.reshape(16, 4, 8, 64) for a in (narrow_ref[...], far_narrow)]
    for g in range(4):
        modes = jnp.concatenate([half[:, g].reshape(128, 64) for half in narrow], 0)
        t_ref[:, g * 8 : (g + 1) * 8, :] = _turn(syn_ref[...], modes).reshape(32, 8, 64)

    def chunk_copy(i):
        at = pl.ds(i * 16, 16)
        return pltpu.make_async_copy(out_ref.at[at], out_any.at[at], sem.at[i])

    def chunk(i, carry):
        hl = hl_ref[:, pl.ds(pl.multiple_of(i * 256, 256), 256)]
        th, tl = _halves(t_ref[pl.ds(i * 4, 4)].reshape(128, 64).T)
        for n in range(4):
            own = slice(32 * n, 32 * n + 32)
            left = jnp.concatenate([th[:, own], th[:, own], tl[:, own], hl[:, n * 64 : (n + 1) * 64]], 1)
            base = _dot(left, wide_ref[...])
            at = pl.ds(i * 16 + 4 * n, 4)
            out_ref[at] = (term_ref[at] + base[None]).astype(BF16)
        chunk_copy(i).start()
        return carry

    lax.fori_loop(0, 8, chunk, 0, unroll=8)
    low_core = place_ref[2] == 0
    scale = 1.0 / 512.0

    def joined(k):
        own = jnp.concatenate([mine_ref[:, :, j, 320:384].reshape(64, 64) for j in (k, k + 1)], 1)
        far = jnp.concatenate([other_ref[:, :, j, 320:384].reshape(64, 64) for j in (k, k + 1)], 1)
        return jnp.where(low_core, jnp.concatenate([own, far], 1), jnp.concatenate([far, own], 1))

    q = joined(0)
    down_out[...] = joined(2) * scale
    fine_out[...] = mine_ref[:, :, 4, 320:384].reshape(64, 64) * (1.0 / 2048.0)
    q_parts = jnp.concatenate(_halves(q), 0)
    tall = lift.astype(F32).T.astype(BF16)
    skip_out[...] = _dot(jnp.concatenate([tall, tall], 1), q_parts) * scale
    lift_sum = _dot_nt(q_parts, skip_ref[...])
    lift_sum = lift_sum[:64] + lift_sum[64:]
    lift_sum += sum_ref[...] + far_sum
    lift_out[...] = lift_sum * scale

    def settle(i, carry):
        chunk_copy(i).wait()
        return carry

    lax.fori_loop(0, 8, settle, 0)


def fine_call(place, *operands):
    vm = pl.BlockSpec(memory_space=pltpu.VMEM)
    return pl.pallas_call(
        _fine_kernel,
        in_specs=[pl.BlockSpec(memory_space=pltpu.SMEM)] + [vm] * 10,
        out_specs=[pl.BlockSpec(memory_space=pl.ANY)] + [vm] * 4,
        out_shape=[
            jax.ShapeDtypeStruct((128, 64, 256), BF16),
            jax.ShapeDtypeStruct((64, 256), F32),
            jax.ShapeDtypeStruct((256, 256), F32),
            jax.ShapeDtypeStruct((64, 256), F32),
            jax.ShapeDtypeStruct((64, 64), F32),
        ],
        scratch_shapes=[
            pltpu.VMEM((32, 32, 64), F32),
            pltpu.VMEM((128, 64, 256), BF16),
            pltpu.SemaphoreType.DMA((8,)),
        ],
        compiler_params=pltpu.CompilerParams(vmem_limit_bytes=VMEM),
        name="fine",
    )(place, *operands)


def other_core(a):
    return lax.ppermute(a, "core", [(0, 1), (1, 0)])


def to_all(copies):
    mine = lax.all_to_all(copies, SAME_CORE, 0, 0, tiled=True)
    mine = mine.reshape(16, 4, 8, -1)
    return mine, other_core(mine)


def body(fine_input, cotangent, lift, weight, skip, down, skip_fine):
    natural, syn_all, ana_all = _row_tables()
    col_down, col_up, col_fine = _col_tables()
    place = jnp.stack([lax.axis_index(ROWS), lax.axis_index(COLS), lax.axis_index("core")]).astype(jnp.int32)
    x = fine_input.transpose(0, 2, 1)
    u = cotangent.transpose(0, 2, 1)
    partial, ps, pst, to_modes, to_grid, to_fine, syn, ana, held = pool_call(
        place, x, natural, col_down, col_up, col_fine, syn_all, ana_all
    )
    got = lax.all_to_all(partial.reshape(128, 4, 128), ALL, 0, 0, tiled=True)
    mixed, p, s = mix_call(place, got, lift, weight)
    mine, other = to_all(mixed)
    su, sut, fine = upstream_call(held, u)
    keep, send, hl = hidden_call(
        place, mine, other, ps, pst, su, sut, lift, skip, down.T, fine, syn, ana, to_grid, to_modes
    )
    far = other_core(send)
    term = term_call(u, skip_fine)
    keep, term = lax.optimization_barrier((keep, term))
    summed = (keep + far).reshape(64, 8, 384)
    got = lax.all_to_all(summed, SAME_CORE, 0, 0, tiled=True)
    pulled, block = adjoint_call(place, got, p, weight)
    mine, other = to_all(block)
    grad_spectral, narrow, lift_sum = outer_call(s, pulled, mine, lift)
    grad_input, g_lift, g_skip, g_down, g_fine = fine_call(
        place, term, hl, mine, narrow, lift_sum, other, lift, skip, syn, to_fine
    )
    return grad_input.transpose(0, 2, 1), grad_spectral, g_lift, g_skip, g_down.T, g_fine


def solution(mesh):
    split = Mesh(mesh.devices.reshape(4, 2, 2, 4, 2), ALL)
    grid = P(ROWS, COLS, None)
    modes = P(None, ALL, None, None)
    return jax.shard_map(
        body,
        mesh=split,
        in_specs=(grid, grid, P(), modes, P(), P(), P()),
        out_specs=(grid, modes, P(), P(), P(), P()),
        check_vma=False,
    )
```

time: 722 us -> 107 us (0.15); the launches traced: 712 us -> 107 us
  waiting for transfers between devices: 441 us -> 1.19 us
  blocking collectives: 130 us -> 76.6 us
  matrix products: 49.2 us -> 0 us
  local copies, waits for them, and re-layouts: 46.7 us -> 0.02 us
  other arithmetic: 29.2 us -> 0.19 us
  Pallas kernels: 0 us -> 22.1 us
  between operations: 15.7 us -> 0.89 us
    unnamed x9 -> x0, waiting for transfers between devices: 164 us -> none
    psum x1 -> x0, waiting for transfers between devices: 134 us -> none  [body(): lax.psum((lift_grad, skip_grad, down_grad, fine_grad), ('rows', 'cols'))]
    reduce_scatter x2 -> x0, waiting for transfers between devices: 119 us -> none  [reduce_modes(): lax.psum_scatter(partial_modes, 'rows', scatter_dimension=1, tiled=True)]
    all_to_all x0 -> x4, blocking collectives: none -> 76.6 us  [the longest x2 34.3 us: to_all(): mine = lax.all_to_all(copies, SAME_CORE, 0, 0, tiled=True)]
    psum x1 -> x0, blocking collectives: 74.6 us -> none  [body(): lax.psum((lift_grad, skip_grad, down_grad, fine_grad), ('rows', 'cols'))]
    all_gather x2 -> x0, blocking collectives: 55.7 us -> none  [spread_modes(): by_cols = lax.all_gather(owned_modes, 'cols', axis=1, tiled=True)]
    dot_general x42 -> x0, matrix products: 49.2 us -> none  [the longest x1 7.91 us: body(): jnp.dot(upstream_flat, skip_fine.T, preferred_element_type=jnp.float32)]
    all_gather x2 -> x0, waiting for transfers between devices: 23.6 us -> none  [spread_modes(): return lax.all_gather(by_cols, 'rows', axis=1, tiled=True)]
  transfers between devices with their start and end apart: 7 -> 3, of which waited for: 6 -> 2; matrix products, arithmetic and copies ran while one was open for 5% -> 0% of each run, Pallas kernels for 0% -> 5%
where the time goes in v1:
time: 107 us
  blocking collectives  76.6 us (72%)
  Pallas kernels  22.1 us (21%)
  starting transfers between devices  6.19 us (6%)
  waiting for transfers between devices  1.19 us (1%)
    all_to_all x2, blocking collectives, to_all(): mine = lax.all_to_all(copies, SAME_CORE, 0, 0, tiled=True)  34.3 us
    all_to_all x1, blocking collectives, body(): got = lax.all_to_all(partial.reshape(128, 4, 128), ALL, 0, 0, tiled=True)  22.6 us
    all_to_all x1, blocking collectives, body(): got = lax.all_to_all(summed, SAME_CORE, 0, 0, tiled=True)  19.7 us
    ppermute x3, starting transfers between devices, other_core(): return lax.ppermute(a, 'core', [(0, 1), (1, 0)])  6.19 us
    pallas_call x1, Pallas kernels, hidden_call(): pl.pallas_call(_hidden_kernel, in_specs=[pl.BlockSpec(memory_space=pltpu....  5.52 us
    pallas_call x1, Pallas kernels, fine_call(): pl.pallas_call(_fine_kernel, in_specs=[pl.BlockSpec(memory_space=pltpu.SM...  4.81 us
    pallas_call x1, Pallas kernels, pool_call(): pl.pallas_call(_pool_kernel, in_specs=[pl.BlockSpec(memory_space=pltpu.SM...  4.61 us
  transfers between devices with their start and end apart: 3, of which 2 were waited for; matrix products, arithmetic and copies ran while one was open for 0% of the time, Pallas kernels for 5%

profile of v1, /device:TPU:1, one launch (start us, length us, event | category | flops | bytes accessed | tf_op | source)
XLA Modules:
  0.0 107.1 jit_solution(15797299842025996606)
XLA Ops:
  0.6 0.1 pad_add_fusion.place_ref
  0.7 0.0 copy-start.1
  0.7 0.0 copy-start.3
  0.7 0.0 copy-start
  0.7 4.6 %pool.1 = (f32[32,4,4,128]{3,2,1,0:T(4,128)S(1)}, bf16[32,64,128]{2,1,0:T(8,128)(2,1)S(1)}, bf16[64,2048]{1,0:T(8,128)(2,1)S(1)}, bf16[64,64]{1,0:T(8,128)(2,1)S...) custom-call(s32[3]{0:T(128)S(1)} %pad_add_fusion.place_ref, ...), custom_call_target="tpu_custom_call" | custom-call | tf_op jit(solution)/shard_map/pool/pallas_call | solution.py:167
  5.3 22.6 %all_to_all.20.got_ref = f32[128,4,128]{2,1,0:T(4,128)S(1)} all-to-all(f32[128,4,128]{2,1,0:T(4,128)S(1)} %bitcast.19), channel_id=1, replica_groups=mesh['z'=4,'xl'=2,'core'=2,'y'=4,'xh'=2] {'z','xl','core','y','xh'}, dimensions={0} | all-to-all | bytes 524288 | tf_op jit(solution)/shard_map/all_to_all | solution.py:540
  27.9 0.0 copy-done.1
  27.9 0.0 copy-done.3
  27.9 1.1 %mix.1 = (f32[64,8,256]{2,1,0:T(8,128)S(1)}, f32[8,64]{1,0:T(8,128)S(1)}, f32[8,256]{1,0:T(8,128)S(1)}) custom-call(s32[3]{0:T(128)S(1)} %pad_add_fusion.place_ref, f32[128,4,128]{2,1,0:T(4,128)S(1)} %all_to_all.20.got_ref, bf16[64,256]{1,0:T(8,128)(2,1)S(1)} %copy-done.3, bf16[2,4,256,256]{3,2,1,0:T(8,128)(2,1)S(1)} %copy-done.1), custom_call_target="tpu_custom_call" | custom-call | tf_op jit(solution)/shard_map/mix/pallas_call | solution.py:247
  29.1 15.7 %all_to_all.21 = f32[64,8,256]{2,1,0:T(8,128)S(1)} all-to-all(f32[64,8,256]{2,1,0:T(8,128)S(1)} %get-tuple-element.37), channel_id=1, replica_groups=mesh['z'=4,'xl'=2,'core'=2,'y'=4,'xh'=2] {'z','xl','y','xh'}, dimensions={0} | all-to-all | bytes 1048576 | tf_op jit(solution)/shard_map/all_to_all | solution.py:526
  44.8 2.6 %collective-permute-start = (f32[16,4,8,256]{3,2,1,0:T(8,128)S(1)}, f32[16,4,8,256]{3,2,1,0:T(8,128)S(1)}, u32[]{:S(2)}, u32[]{:S(2)}) collective-permute-start(f32[16,4,8,256]{3,2,1,0:T(8,128)S(1)} %bitcast.17), channel_id=1, source_target_pairs={{0,8},{8,0},{1,9},{9,1},{2,10},{10,2},{3,11},{11,3},{4,12},{12,4},... | collective-permute-start | bytes 1572872 | tf_op jit(solution)/shard_map/ppermute | solution.py:522
  47.4 0.0 copy-done
  47.4 0.0 copy-start.2
  47.4 0.0 copy-start.4
  47.4 0.0 copy-start.5
  47.4 2.1 %upstream.1 = (bf16[32,64,64]{2,1,0:T(8,128)(2,1)S(1)}, bf16[64,2048]{1,0:T(8,128)(2,1)S(1)}, f32[64,64]{1,0:T(8,128)S(1)}) custom-call(bf16[128,64,256]{2,1,0:T(8,128)(2,1)S(1)} %get-tuple-element.40.x_ref, bf16[128,64,256]{2,1,0:T(8,128)(2,1)S(1)} %bitcast.12), custom_call_target="tpu_custom_call" | custom-call | tf_op jit(solution)/shard_map/upstream/pallas_call | solution.py:210
  49.4 0.0 collective-permute-done.other_ref
  49.5 0.0 copy-done.2
  49.5 0.0 copy-done.4
  49.5 5.5 %hidden.1 = (f32[16,4,8,384]{3,2,1,0:T(8,128)S(1)}, f32[16,4,8,384]{3,2,1,0:T(8,128)S(1)}, bf16[64,2048]{1,0:T(8,128)(2,1)S(1)}) custom-call(s32[3]{0:T(128)S(1)} %pad_add_fusion.place_ref, f32[16,4,8,256]{3,2,1,0:T(8,128)S(1)} %bitcast.18, f32[16,4,8,256]{3,2,1,0:T(8,128)S(1)} %collective-permute-done.other_ref, ...), custom_call_target="tpu_custom_call" | custom-call | tf_op jit(solution)/shard_map/hidden/pallas_call | solution.py:324
  55.0 0.1 collective-permute-start.1
  55.1 0.0 copy-done.5
  55.1 1.3 %term.1.term_ref = f32[128,64,256]{2,1,0:T(8,128)S(1)} custom-call(bf16[128,64,256]{2,1,0:T(8,128)(2,1)S(1)} %bitcast.13, bf16[64,64]{1,0:T(8,128)(2,1)S(1)} %copy-done.5), custom_call_target="tpu_custom_call" | custom-call | flops 400000000 | bytes 12000000 | tf_op jit(solution)/shard_map/term/pallas_call | solution.py:433
  56.4 1.0 collective-permute-done.1
  57.4 0.1 add.15
  57.5 19.7 %all_to_all.22.got_ref = f32[64,8,384]{2,1,0:T(8,128)S(1)} all-to-all(f32[64,8,384]{2,1,0:T(8,128)S(1)} %bitcast.22), channel_id=1, replica_groups=mesh['z'=4,'xl'=2,'core'=2,'y'=4,'xh'=2] {'z','xl','y','xh'}, dimensions={0} | all-to-all | bytes 1572864 | tf_op jit(solution)/shard_map/all_to_all | solution.py:551
  77.2 1.0 adjoint.1
  78.2 18.6 %all_to_all.23 = f32[64,8,384]{2,1,0:T(8,128)S(1)} all-to-all(f32[64,8,384]{2,1,0:T(8,128)S(1)} %get-tuple-element.54), channel_id=1, replica_groups=mesh['z'=4,'xl'=2,'core'=2,'y'=4,'xh'=2] {'z','xl','y','xh'}, dimensions={0} | all-to-all | bytes 1572864 | tf_op jit(solution)/shard_map/all_to_all | solution.py:526
  96.8 3.5 %collective-permute-start.2 = (f32[16,4,8,384]{3,2,1,0:T(8,128)S(1)}, f32[16,4,8,384]{3,2,1,0:T(8,128)S(1)}, u32[]{:S(2)}, u32[]{:S(2)}) collective-permute-start(f32[16,4,8,384]{3,2,1,0:T(8,128)S(1)} %bitcast.14), channel_id=1, source_target_pairs={{0,8},{8,0},{1,9},{9,1},{2,10},{10,2},{3,11},{11,3},{4,12},{12,4},... | collective-permute-start | bytes 2359304 | tf_op jit(solution)/shard_map/ppermute | solution.py:522
  100.3 1.7 %outer.1 = (f32[2,4,256,256]{3,2,1,0:T(8,128)}, f32[512,64]{1,0:T(8,128)S(1)}, f32[64,256]{1,0:T(8,128)S(1)}) custom-call(f32[8,256]{1,0:T(8,128)S(1)} %get-tuple-element.55.s_ref, f32[8,256]{1,0:T(8,128)S(1)} %get-tuple-element.56.pulled_ref, f32[16,4,8,384]{3,2,1,0:T(8,128)S(1)} %bitcast.15, bf16[64,256]{1,0:T(8,128)(2,1)S(1)} %copy-done.3), custom_call_target="tpu_custom_call" | custom-call | flops 2000000 | bytes 2200000 | tf_op jit(solution)/shard_map/outer/pallas_call | solution.py:405
  101.9 0.2 collective-permute-done.2.other_ref
  102.2 4.8 %fine.1 = (bf16[128,64,256]{2,1,0:T(8,128)(2,1)}, f32[64,256]{1,0:T(8,128)}, f32[256,256]{1,0:T(8,128)}, f32[64,256]{1,0:T(8,128)}, f32[64,64]{1,0:T(8,128)}) custom-call(s32[3]{0:T(128)S(1)} %pad_add_fusion.place_ref, f32[128,64,256]{2,1,0:T(8,128)S(1)} %term.1.term_ref, bf16[64,2048]{1,0:T(8,128)(2,1)S(1)} %get-tuple-element.50.hl_ref, ...), custom_call_target="tpu_custom_call" | custom-call | tf_op jit(solution)/shard_map/fine/pallas_call | solution.py:500
Async XLA Ops:
  0.7 27.2 %copy-start.1 = (bf16[2,4,256,256]{3,2,1,0:T(8,128)(2,1)S(1)}, bf16[2,4,256,256]{3,2,1,0:T(8,128)(2,1)}, u32[]{:S(2)}) copy-start(bf16[2,4,256,256]{3,2,1,0:T(8,128)(2,1)} %w_ref.3) | copy-start | bytes 3145732
  0.7 27.2 %copy-start.3 = (bf16[64,256]{1,0:T(8,128)(2,1)S(1)}, bf16[64,256]{1,0:T(8,128)(2,1)}, u32[]{:S(2)}) copy-start(bf16[64,256]{1,0:T(8,128)(2,1)} %lift_ref.7) | copy-start | bytes 98308
  0.7 46.6 %copy-start = (bf16[128,256,64]{1,2,0:T(8,128)(2,1)S(1)}, bf16[128,256,64]{1,2,0:T(8,128)(2,1)}, u32[]{:S(2)}) copy-start(bf16[128,256,64]{1,2,0:T(8,128)(2,1)} %param.14) | copy-start | bytes 12582916
  44.8 4.7 %collective-permute-start = (f32[16,4,8,256]{3,2,1,0:T(8,128)S(1)}, f32[16,4,8,256]{3,2,1,0:T(8,128)S(1)}, u32[]{:S(2)}, u32[]{:S(2)}) collective-permute-start(f32[16,4,8,256]{3,2,1,0:T(8,128)S(1)} %bitcast.17), channel_id=1, source_target_pairs={{0,8},{8,0},{1,9},{9,1},{2,10},{10,2},{3,11},{11,3},{4,12},{12,4},... | collective-permute-start | bytes 1572872 | tf_op jit(solution)/shard_map/ppermute | solution.py:522
  47.4 2.1 %copy-start.2 = (bf16[256,256]{1,0:T(8,128)(2,1)S(1)}, bf16[256,256]{1,0:T(8,128)(2,1)}, u32[]{:S(2)}) copy-start(bf16[256,256]{1,0:T(8,128)(2,1)} %skip_ref.3) | copy-start | bytes 393220
  47.4 2.1 %copy-start.4 = (bf16[256,64]{0,1:T(8,128)(2,1)S(1)}, bf16[256,64]{0,1:T(8,128)(2,1)}, u32[]{:S(2)}) copy-start(bf16[256,64]{0,1:T(8,128)(2,1)} %param.18) | copy-start | bytes 98308
  47.4 7.7 %copy-start.5 = (bf16[64,64]{1,0:T(8,128)(2,1)S(1)}, bf16[64,64]{1,0:T(8,128)(2,1)}, u32[]{:S(2)}) copy-start(bf16[64,64]{1,0:T(8,128)(2,1)} %sf_ref.1) | copy-start | bytes 24580
  55.0 2.4 %collective-permute-start.1 = (f32[16,4,8,384]{3,2,1,0:T(8,128)S(1)}, f32[16,4,8,384]{3,2,1,0:T(8,128)S(1)}, u32[]{:S(2)}, u32[]{:S(2)}) collective-permute-start(f32[16,4,8,384]{3,2,1,0:T(8,128)S(1)} %get-tuple-element.52), channel_id=1, source_target_pairs={{0,8},{8,0},{1,9},{9,1},{2,10},{10,2},{3,11},{11,3},{4,12},{12,4},... | collective-permute-start | bytes 2359304 | tf_op jit(solution)/shard_map/ppermute | solution.py:522
  96.8 5.4 %collective-permute-start.2 = (f32[16,4,8,384]{3,2,1,0:T(8,128)S(1)}, f32[16,4,8,384]{3,2,1,0:T(8,128)S(1)}, u32[]{:S(2)}, u32[]{:S(2)}) collective-permute-start(f32[16,4,8,384]{3,2,1,0:T(8,128)S(1)} %bitcast.14), channel_id=1, source_target_pairs={{0,8},{8,0},{1,9},{9,1},{2,10},{10,2},{3,11},{11,3},{4,12},{12,4},... | collective-permute-start | bytes 2359304 | tf_op jit(solution)/shard_map/ppermute | solution.py:522

commit v2 on v1

--- a/solution.py
+++ b/solution.py
@@ -15,7 +15,7 @@
 ROWS = ("z", "xl", "core")
 COLS = ("y", "xh")
 ALL = ROWS + COLS
-SAME_CORE = ("z", "xl", "y", "xh")
+SAME_CORE = COLS + ("z", "xl")
 
 PERIOD = 576
 N_R, N_C = 16, 8
@@ -41,7 +41,7 @@
     full = np.einsum("rjpnq,ts->rjptnqs", m, np.eye(4))
     natural = full.transpose(0, 2, 1, 3, 4, 5, 6).reshape(N_R, 256, 256)
     split = full.reshape(N_R, 8, 2, 2, 2, 4, 256)
-    split = split.transpose(0, 2, 1, 3, 4, 5, 6)
+    split = split.transpose(0, 2, 3, 1, 4, 5, 6)
     by_core = np.stack([split[r, [r & 1, 1 - (r & 1)]] for r in range(N_R)])
     by_core = by_core.reshape(N_R, 256, 256)
     return tuple(
@@ -302,18 +302,19 @@
     lax.fori_loop(0, 8, group, 0, unroll=8)
     for g in range(4):
         done = _turn(ana_ref[...], c_ref[g])
-        keep_ref[:, g, :, 0:256] = done[:128].reshape(16, 8, 256)
-        send_ref[:, g, :, 0:256] = done[128:].reshape(16, 8, 256)
+        for ref, mine in ((keep_ref, done[:128]), (send_ref, done[128:])):
+            mine = mine.reshape(2, 8, 8, 256)
+            for k in range(4):
+                lanes, rows = 128 * (k // 2), 4 * (k % 2)
+                ref[:, g, :, k] = mine[:, :, rows : rows + 4, lanes : lanes + 128]
     core = place_ref[2]
-    blank = jnp.zeros((64, 64), F32)
+    fine = jnp.concatenate([fine_ref[...], jnp.zeros((64, 64), F32)], 1)
 
     def extras(ref, low_half):
-        ref[:, :, :, 256:384] = jnp.zeros((16, 4, 8, 128), F32)
         q = jnp.where(low_half, q_ref[:, 0:128], q_ref[:, 128:256])
         d = jnp.where(low_half, d_ref[:, 0:128], d_ref[:, 128:256])
-        planes = [q[:, :64], q[:, 64:], d[:, :64], d[:, 64:], fine_ref[...]]
-        for k, plane in enumerate(planes):
-            ref[:, :, k, 256:384] = jnp.concatenate([blank, plane], 1).reshape(16, 4, 128)
+        for k, plane in enumerate((q, d, fine, jnp.zeros((64, 128), F32))):
+            ref[:, :, :, 4, k, :] = plane.reshape(2, 4, 8, 128)
 
     extras(keep_ref, core == 0)
     extras(send_ref, core == 1)
@@ -326,8 +327,8 @@
         in_specs=[pl.BlockSpec(memory_space=pltpu.SMEM)] + [vm] * 14,
         out_specs=[vm] * 3,
         out_shape=[
-            jax.ShapeDtypeStruct((16, 4, 8, 384), F32),
-            jax.ShapeDtypeStruct((16, 4, 8, 384), F32),
+            jax.ShapeDtypeStruct((2, 4, 8, 5, 4, 128), F32),
+            jax.ShapeDtypeStruct((2, 4, 8, 5, 4, 128), F32),
             jax.ShapeDtypeStruct((64, 2048), BF16),
         ],
         scratch_shapes=[
@@ -343,7 +344,12 @@
 
 def _adjoint_kernel(place_ref, got_ref, p_ref, w_ref, pulled_ref, block_ref):
     total = got_ref[...].sum(0)
-    pulled = total[:, :256] * _mode_weight(place_ref)
+    pulled = jnp.concatenate([jnp.concatenate([total[k], total[k + 1]], 0) for k in (0, 2)], 1)
+    pulled = pulled * _mode_weight(place_ref)
+    sums = total[4]
+    sums = jnp.concatenate(
+        [sums[0:1, :64], sums[0:1, 64:], sums[1:2, :64], sums[1:2, 64:], sums[2:3, :64], jnp.zeros((3, 64), F32)], 0
+    )
     pulled_ref[...] = pulled
     parts = jnp.concatenate(_halves(pulled), 0)
     row = lax.broadcasted_iota(jnp.int32, (8, 256), 0)
@@ -356,7 +362,7 @@
         b = b[:8] + b[8:]
         b = jnp.concatenate([b[4:], b[:4]], 0)
         back = jnp.where(lax.rem(row, 4) == t, a + sign * b, back)
-    block = jnp.concatenate([back, p_ref[...], total[:, 320:384]], 1)
+    block = jnp.concatenate([back, p_ref[...], sums], 1)
     block_ref[...] = jnp.broadcast_to(block[None], (64, 8, 384))
 
 
@@ -376,9 +382,9 @@
 
 
 def _gathered(ref, lift):
-    high, low = _halves(ref[:, :, :, 0:256].reshape(512, 256))
+    high, low = _halves(ref[:, :, :, :, 0:256].reshape(512, 256))
     narrow = _dot_nt(high, lift) + _dot_nt(low, lift)
-    p_high, p_low = _halves(ref[:, :, :, 256:384].reshape(512, 128).T[:64])
+    p_high, p_low = _halves(ref[:, :, :, :, 256:384].reshape(512, 128).T[:64])
     both = _dot(jnp.concatenate([p_high, p_low], 0), high)
     return narrow, both[:64] + both[64:] + _dot(p_high, low)
 
@@ -447,7 +453,7 @@
 ):
     lift = lift_ref[...]
     far_narrow, far_sum = _gathered(other_ref, lift)
-    narrow = [a.reshape(16, 4, 8, 64) for a in (narrow_ref[...], far_narrow)]
+    narrow = [a.reshape(2, 4, 8, 8, 64) for a in (narrow_ref[...], far_narrow)]
     for g in range(4):
         modes = jnp.concatenate([half[:, g].reshape(128, 64) for half in narrow], 0)
         t_ref[:, g * 8 : (g + 1) * 8, :] = _turn(syn_ref[...], modes).reshape(32, 8, 64)
@@ -473,13 +479,13 @@
     scale = 1.0 / 512.0
 
     def joined(k):
-        own = jnp.concatenate([mine_ref[:, :, j, 320:384].reshape(64, 64) for j in (k, k + 1)], 1)
-        far = jnp.concatenate([other_ref[:, :, j, 320:384].reshape(64, 64) for j in (k, k + 1)], 1)
+        own = jnp.concatenate([mine_ref[:, :, :, j, 320:384].reshape(64, 64) for j in (k, k + 1)], 1)
+        far = jnp.concatenate([other_ref[:, :, :, j, 320:384].reshape(64, 64) for j in (k, k + 1)], 1)
         return jnp.where(low_core, jnp.concatenate([own, far], 1), jnp.concatenate([far, own], 1))
 
     q = joined(0)
     down_out[...] = joined(2) * scale
-    fine_out[...] = mine_ref[:, :, 4, 320:384].reshape(64, 64) * (1.0 / 2048.0)
+    fine_out[...] = mine_ref[:, :, :, 4, 320:384].reshape(64, 64) * (1.0 / 2048.0)
     q_parts = jnp.concatenate(_halves(q), 0)
     tall = lift.astype(F32).T.astype(BF16)
     skip_out[...] = _dot(jnp.concatenate([tall, tall], 1), q_parts) * scale
@@ -524,7 +530,7 @@
 
 def to_all(copies):
     mine = lax.all_to_all(copies, SAME_CORE, 0, 0, tiled=True)
-    mine = mine.reshape(16, 4, 8, -1)
+    mine = mine.reshape(2, 4, 8, 8, -1)
     return mine, other_core(mine)
 
 
@@ -547,8 +553,8 @@
     far = other_core(send)
     term = term_call(u, skip_fine)
     keep, term = lax.optimization_barrier((keep, term))
-    summed = (keep + far).reshape(64, 8, 384)
-    got = lax.all_to_all(summed, SAME_CORE, 0, 0, tiled=True)
+    summed = (keep + far).reshape(320, 4, 128)
+    got = lax.all_to_all(summed, SAME_CORE, 0, 0, tiled=True).reshape(64, 5, 4, 128)
     pulled, block = adjoint_call(place, got, p, weight)
     mine, other = to_all(block)
     grad_spectral, narrow, lift_sum = outer_call(s, pulled, mine, lift)

time: 107 us -> 105 us (0.981)
  blocking collectives: 76.6 us -> 74.8 us
    all_to_all x1, blocking collectives: 19.7 us -> 18.3 us  [body(): lax.all_to_all(summed, SAME_CORE, 0, 0, tiled=True).reshape(64, 5, 4, 128)]
where the time goes in v2:
time: 105 us
  blocking collectives  74.8 us (71%)
  Pallas kernels  22.1 us (21%)
  starting transfers between devices  5.98 us (6%)
    all_to_all x2, blocking collectives, to_all(): mine = lax.all_to_all(copies, SAME_CORE, 0, 0, tiled=True)  33.9 us
    all_to_all x1, blocking collectives, body(): got = lax.all_to_all(partial.reshape(128, 4, 128), ALL, 0, 0, tiled=True)  22.6 us
    all_to_all x1, blocking collectives, body(): lax.all_to_all(summed, SAME_CORE, 0, 0, tiled=True).reshape(64, 5, 4, 128)  18.3 us
    ppermute x3, starting transfers between devices, other_core(): return lax.ppermute(a, 'core', [(0, 1), (1, 0)])  5.98 us
    pallas_call x1, Pallas kernels, hidden_call(): pl.pallas_call(_hidden_kernel, in_specs=[pl.BlockSpec(memory_space=pltpu....  5.51 us
    pallas_call x1, Pallas kernels, fine_call(): pl.pallas_call(_fine_kernel, in_specs=[pl.BlockSpec(memory_space=pltpu.SM...  4.77 us
    pallas_call x1, Pallas kernels, pool_call(): pl.pallas_call(_pool_kernel, in_specs=[pl.BlockSpec(memory_space=pltpu.SM...  4.61 us
  transfers between devices with their start and end apart: 3, of which 2 were waited for; matrix products, arithmetic and copies ran while one was open for 0% of the time, Pallas kernels for 5%

profile of v2, /device:TPU:1, one launch (start us, length us, event | category | flops | bytes accessed | tf_op | source)
XLA Modules:
  0.0 105.1 jit_solution(14700569572507825704)
XLA Ops:
  0.6 0.1 pad_add_fusion.place_ref
  0.7 0.0 copy-start.1
  0.7 0.0 copy-start.3
  0.7 0.0 copy-start
  0.7 4.6 %pool.1 = (f32[32,4,4,128]{3,2,1,0:T(4,128)S(1)}, bf16[32,64,128]{2,1,0:T(8,128)(2,1)S(1)}, bf16[64,2048]{1,0:T(8,128)(2,1)S(1)}, bf16[64,64]{1,0:T(8,128)(2,1)S...) custom-call(s32[3]{0:T(128)S(1)} %pad_add_fusion.place_ref, ...), custom_call_target="tpu_custom_call" | custom-call | tf_op jit(solution)/shard_map/pool/pallas_call | solution.py:167
  5.3 22.6 %all_to_all.20.got_ref = f32[128,4,128]{2,1,0:T(4,128)S(1)} all-to-all(f32[128,4,128]{2,1,0:T(4,128)S(1)} %bitcast.21), channel_id=1, replica_groups=mesh['z'=4,'xl'=2,'core'=2,'y'=4,'xh'=2] {'z','xl','core','y','xh'}, dimensions={0} | all-to-all | bytes 524288 | tf_op jit(solution)/shard_map/all_to_all | solution.py:546
  27.9 0.0 copy-done.1
  27.9 0.0 copy-done.3
  27.9 1.1 %mix.1 = (f32[64,8,256]{2,1,0:T(8,128)S(1)}, f32[8,64]{1,0:T(8,128)S(1)}, f32[8,256]{1,0:T(8,128)S(1)}) custom-call(s32[3]{0:T(128)S(1)} %pad_add_fusion.place_ref, f32[128,4,128]{2,1,0:T(4,128)S(1)} %all_to_all.20.got_ref, bf16[64,256]{1,0:T(8,128)(2,1)S(1)} %copy-done.3, bf16[2,4,256,256]{3,2,1,0:T(8,128)(2,1)S(1)} %copy-done.1), custom_call_target="tpu_custom_call" | custom-call | tf_op jit(solution)/shard_map/mix/pallas_call | solution.py:247
  29.1 15.9 %all_to_all.21 = f32[64,8,256]{2,1,0:T(8,128)S(1)} all-to-all(f32[64,8,256]{2,1,0:T(8,128)S(1)} %get-tuple-element.37), channel_id=1, replica_groups=mesh['z'=4,'xl'=2,'core'=2,'y'=4,'xh'=2] {'y','xh','z','xl'}, dimensions={0} | all-to-all | bytes 1048576 | tf_op jit(solution)/shard_map/all_to_all | solution.py:532
  45.0 2.5 %collective-permute-start = (f32[2,4,8,8,256]{4,3,2,1,0:T(8,128)S(1)}, f32[2,4,8,8,256]{4,3,2,1,0:T(8,128)S(1)}, u32[]{:S(2)}, u32[]{:S(2)}) collective-permute-start(f32[2,4,8,8,256]{4,3,2,1,0:T(8,128)S(1)} %bitcast.19), channel_id=1, source_target_pairs={{0,8},{8,0},{1,9},{9,1},{2,10},{10,2},{3,11},{11,3},{4,12},{12,4},... | collective-permute-start | bytes 1572872 | tf_op jit(solution)/shard_map/ppermute | solution.py:528
  47.5 0.0 copy-done
  47.5 0.0 copy-start.2
  47.5 0.0 copy-start.4
  47.5 0.0 copy-start.5
  47.5 2.1 %upstream.1 = (bf16[32,64,64]{2,1,0:T(8,128)(2,1)S(1)}, bf16[64,2048]{1,0:T(8,128)(2,1)S(1)}, f32[64,64]{1,0:T(8,128)S(1)}) custom-call(bf16[128,64,256]{2,1,0:T(8,128)(2,1)S(1)} %get-tuple-element.40.x_ref, bf16[128,64,256]{2,1,0:T(8,128)(2,1)S(1)} %bitcast.13), custom_call_target="tpu_custom_call" | custom-call | tf_op jit(solution)/shard_map/upstream/pallas_call | solution.py:210
  49.5 0.0 collective-permute-done.other_ref
  49.6 0.0 copy-done.2
  49.6 0.0 copy-done.4
  49.6 5.5 %hidden.1 = (f32[2,4,8,5,4,128]{5,4,3,2,1,0:T(4,128)S(1)}, f32[2,4,8,5,4,128]{5,4,3,2,1,0:T(4,128)S(1)}, bf16[64,2048]{1,0:T(8,128)(2,1)S(1)}) custom-call(s32[3]{0:T(128)S(1)} %pad_add_fusion.place_ref, f32[2,4,8,8,256]{4,3,2,1,0:T(8,128)S(1)} %bitcast.20, f32[2,4,8,8,256]{4,3,2,1,0:T(8,128)S(1)} %collective-permute-done.other_ref, ...), custom_call_target="tpu_custom_call" | custom-call | tf_op jit(solution)/shard_map/hidden/pallas_call | solution.py:325
  55.1 0.1 collective-permute-start.1
  55.2 0.0 copy-done.5
  55.2 1.3 %term.1.term_ref = f32[128,64,256]{2,1,0:T(8,128)S(1)} custom-call(bf16[128,64,256]{2,1,0:T(8,128)(2,1)S(1)} %bitcast.14, bf16[64,64]{1,0:T(8,128)(2,1)S(1)} %copy-done.5), custom_call_target="tpu_custom_call" | custom-call | flops 400000000 | bytes 12000000 | tf_op jit(solution)/shard_map/term/pallas_call | solution.py:439
  56.5 0.8 collective-permute-done.1
  57.3 0.2 add.15
  57.5 18.3 %all_to_all.22 = f32[320,4,128]{2,1,0:T(4,128)S(1)} all-to-all(f32[320,4,128]{2,1,0:T(4,128)S(1)} %bitcast.24), channel_id=1, replica_groups=mesh['z'=4,'xl'=2,'core'=2,'y'=4,'xh'=2] {'y','xh','z','xl'}, dimensions={0} | all-to-all | bytes 1310720 | tf_op jit(solution)/shard_map/all_to_all | solution.py:557
  75.7 1.1 %adjoint.1 = (f32[8,256]{1,0:T(8,128)S(1)}, f32[64,8,384]{2,1,0:T(8,128)S(1)}) custom-call(s32[3]{0:T(128)S(1)} %pad_add_fusion.place_ref, f32[64,5,4,128]{3,2,1,0:T(4,128)S(1)} %bitcast.18, f32[8,64]{1,0:T(8,128)S(1)} %get-tuple-element.53.p_ref, bf16[2,4,256,256]{3,2,1,0:T(8,128)(2,1)S(1)} %copy-done.1), custom_call_target="tpu_custom_call" | custom-call | tf_op jit(solution)/shard_map/adjoint/pallas_call | solution.py:371
  76.8 18.0 %all_to_all.23 = f32[64,8,384]{2,1,0:T(8,128)S(1)} all-to-all(f32[64,8,384]{2,1,0:T(8,128)S(1)} %get-tuple-element.54), channel_id=1, replica_groups=mesh['z'=4,'xl'=2,'core'=2,'y'=4,'xh'=2] {'y','xh','z','xl'}, dimensions={0} | all-to-all | bytes 1572864 | tf_op jit(solution)/shard_map/all_to_all | solution.py:532
  94.8 3.4 %collective-permute-start.2 = (f32[2,4,8,8,384]{4,3,2,1,0:T(8,128)S(1)}, f32[2,4,8,8,384]{4,3,2,1,0:T(8,128)S(1)}, u32[]{:S(2)}, u32[]{:S(2)}) collective-permute-start(f32[2,4,8,8,384]{4,3,2,1,0:T(8,128)S(1)} %bitcast.15), channel_id=1, source_target_pairs={{0,8},{8,0},{1,9},{9,1},{2,10},{10,2},{3,11},{11,3},{4,12},{12,4},... | collective-permute-start | bytes 2359304 | tf_op jit(solution)/shard_map/ppermute | solution.py:528
  98.2 1.7 %outer.1 = (f32[2,4,256,256]{3,2,1,0:T(8,128)}, f32[512,64]{1,0:T(8,128)S(1)}, f32[64,256]{1,0:T(8,128)S(1)}) custom-call(f32[8,256]{1,0:T(8,128)S(1)} %get-tuple-element.55.s_ref, f32[8,256]{1,0:T(8,128)S(1)} %get-tuple-element.56.pulled_ref, f32[2,4,8,8,384]{4,3,2,1,0:T(8,128)S(1)} %bitcast.16, bf16[64,256]{1,0:T(8,128)(2,1)S(1)} %copy-done.3), custom_call_target="tpu_custom_call" | custom-call | flops 2000000 | bytes 2200000 | tf_op jit(solution)/shard_map/outer/pallas_call | solution.py:411
  99.9 0.2 collective-permute-done.2.other_ref
  100.1 4.8 %fine.1 = (bf16[128,64,256]{2,1,0:T(8,128)(2,1)}, f32[64,256]{1,0:T(8,128)}, f32[256,256]{1,0:T(8,128)}, f32[64,256]{1,0:T(8,128)}, f32[64,64]{1,0:T(8,128)}) custom-call(s32[3]{0:T(128)S(1)} %pad_add_fusion.place_ref, f32[128,64,256]{2,1,0:T(8,128)S(1)} %term.1.term_ref, bf16[64,2048]{1,0:T(8,128)(2,1)S(1)} %get-tuple-element.50.hl_ref, ...), custom_call_target="tpu_custom_call" | custom-call | tf_op jit(solution)/shard_map/fine/pallas_call | solution.py:506
Async XLA Ops:
  0.7 27.2 %copy-start.1 = (bf16[2,4,256,256]{3,2,1,0:T(8,128)(2,1)S(1)}, bf16[2,4,256,256]{3,2,1,0:T(8,128)(2,1)}, u32[]{:S(2)}) copy-start(bf16[2,4,256,256]{3,2,1,0:T(8,128)(2,1)} %w_ref.3) | copy-start | bytes 3145732
  0.7 27.2 %copy-start.3 = (bf16[64,256]{1,0:T(8,128)(2,1)S(1)}, bf16[64,256]{1,0:T(8,128)(2,1)}, u32[]{:S(2)}) copy-start(bf16[64,256]{1,0:T(8,128)(2,1)} %lift_ref.7) | copy-start | bytes 98308
  0.7 46.7 %copy-start = (bf16[128,256,64]{1,2,0:T(8,128)(2,1)S(1)}, bf16[128,256,64]{1,2,0:T(8,128)(2,1)}, u32[]{:S(2)}) copy-start(bf16[128,256,64]{1,2,0:T(8,128)(2,1)} %param.14) | copy-start | bytes 12582916
  45.0 4.6 %collective-permute-start = (f32[2,4,8,8,256]{4,3,2,1,0:T(8,128)S(1)}, f32[2,4,8,8,256]{4,3,2,1,0:T(8,128)S(1)}, u32[]{:S(2)}, u32[]{:S(2)}) collective-permute-start(f32[2,4,8,8,256]{4,3,2,1,0:T(8,128)S(1)} %bitcast.19), channel_id=1, source_target_pairs={{0,8},{8,0},{1,9},{9,1},{2,10},{10,2},{3,11},{11,3},{4,12},{12,4},... | collective-permute-start | bytes 1572872 | tf_op jit(solution)/shard_map/ppermute | solution.py:528
  47.5 2.1 %copy-start.2 = (bf16[256,256]{1,0:T(8,128)(2,1)S(1)}, bf16[256,256]{1,0:T(8,128)(2,1)}, u32[]{:S(2)}) copy-start(bf16[256,256]{1,0:T(8,128)(2,1)} %skip_ref.3) | copy-start | bytes 393220
  47.5 2.1 %copy-start.4 = (bf16[256,64]{0,1:T(8,128)(2,1)S(1)}, bf16[256,64]{0,1:T(8,128)(2,1)}, u32[]{:S(2)}) copy-start(bf16[256,64]{0,1:T(8,128)(2,1)} %param.18) | copy-start | bytes 98308
  47.5 7.7 %copy-start.5 = (bf16[64,64]{1,0:T(8,128)(2,1)S(1)}, bf16[64,64]{1,0:T(8,128)(2,1)}, u32[]{:S(2)}) copy-start(bf16[64,64]{1,0:T(8,128)(2,1)} %sf_ref.1) | copy-start | bytes 24580
  55.1 2.2 %collective-permute-start.1 = (f32[2,4,8,5,4,128]{5,4,3,2,1,0:T(4,128)S(1)}, f32[2,4,8,5,4,128]{5,4,3,2,1,0:T(4,128)S(1)}, u32[]{:S(2)}, u32[]{:S(2)}) collective-permute-start(f32[2,4,8,5,4,128]{5,4,3,2,1,0:T(4,128)S(1)} %get-tuple-element.52), channel_id=1, source_target_pairs={{0,8},{8,0},{1,9},{9,1},{2,10},{10,2},{3,11},{11,3},{4,12},{12,4},... | collective-permute-start | bytes 1966088 | tf_op jit(solution)/shard_map/ppermute | solution.py:528
  94.8 5.3 %collective-permute-start.2 = (f32[2,4,8,8,384]{4,3,2,1,0:T(8,128)S(1)}, f32[2,4,8,8,384]{4,3,2,1,0:T(8,128)S(1)}, u32[]{:S(2)}, u32[]{:S(2)}) collective-permute-start(f32[2,4,8,8,384]{4,3,2,1,0:T(8,128)S(1)} %bitcast.15), channel_id=1, source_target_pairs={{0,8},{8,0},{1,9},{9,1},{2,10},{10,2},{3,11},{11,3},{4,12},{12,4},... | collective-permute-start | bytes 2359304 | tf_op jit(solution)/shard_map/ppermute | solution.py:528

commit v3 on v2

--- a/solution.py
+++ b/solution.py
@@ -260,7 +260,7 @@
 
 def _hidden_kernel(
     place_ref, mine_ref, other_ref, ps_ref, pst_ref, su_ref, sut_ref, lift_ref, skip_ref, downt_ref, fine_ref,
-    syn_ref, ana_ref, up_ref, down_ref, keep_ref, send_ref, hl_ref, t_ref, c_ref, q_ref, d_ref,
+    syn_ref, ana_ref, up_ref, down_ref, keep_ref, send_ref, hg_ref, both_ref, t_ref, c_ref, q_ref, d_ref,
 ):
     for g in range(4):
         modes = jnp.concatenate([mine_ref[:, g].reshape(128, 256), other_ref[:, g].reshape(128, 256)], 0)
@@ -268,6 +268,7 @@
         t_ref[:, g * 8 : (g + 1) * 8, :] = turned.reshape(32, 8, 256)
     both = _dot(lift_ref[...], skip_ref[...])
     high, low = _halves(both)
+    both_ref[...] = high
     right = jnp.concatenate([high, low], 0)
     downt = downt_ref[...]
     q_ref[...] = jnp.zeros((64, 256), F32)
@@ -296,7 +297,7 @@
             at = pl.multiple_of((i * 4 + n) * 8, 8)
             for g in range(4):
                 c_ref[g, pl.ds(at, 8), :] = modes[g * 8 : (g + 1) * 8]
-        hl_ref[:, lanes] = _dot_nt(high, hg).astype(BF16)
+        hg_ref[lanes, :] = hg
         return carry
 
     lax.fori_loop(0, 8, group, 0, unroll=8)
@@ -325,11 +326,12 @@
     return pl.pallas_call(
         _hidden_kernel,
         in_specs=[pl.BlockSpec(memory_space=pltpu.SMEM)] + [vm] * 14,
-        out_specs=[vm] * 3,
+        out_specs=[vm] * 4,
         out_shape=[
             jax.ShapeDtypeStruct((2, 4, 8, 5, 4, 128), F32),
             jax.ShapeDtypeStruct((2, 4, 8, 5, 4, 128), F32),
-            jax.ShapeDtypeStruct((64, 2048), BF16),
+            jax.ShapeDtypeStruct((2048, 256), BF16),
+            jax.ShapeDtypeStruct((64, 256), BF16),
         ],
         scratch_shapes=[
             pltpu.VMEM((32, 32, 256), F32),
@@ -424,27 +426,30 @@
     )(s, pulled, mine, lift)
 
 
-def _term_kernel(u_ref, sf_ref, out_ref):
+def _term_kernel(u_ref, sf_ref, hg_ref, both_ref, out_ref, hl_ref):
     row = lax.broadcasted_iota(jnp.int32, (256, 256), 0)
     col = lax.broadcasted_iota(jnp.int32, (256, 256), 1)
     sf = sf_ref[...].astype(F32)
     sf = jnp.concatenate([jnp.concatenate([sf] * 4, 1)] * 4, 0)
     sf = jnp.where(row // 64 == col // 64, sf, 0.0).astype(BF16)
+    for i in range(8):
+        at = slice(256 * i, 256 * (i + 1))
+        hl_ref[:, at] = _dot_nt(both_ref[...], hg_ref[at, :]).astype(BF16)
     for n in range(32):
         out_ref[4 * n : 4 * n + 4] = _dot(sf, u_ref[4 * n : 4 * n + 4].reshape(256, 256)).reshape(4, 64, 256)
 
 
-def term_call(u, sf):
+def term_call(u, sf, hg, both):
     vm = pl.BlockSpec(memory_space=pltpu.VMEM)
     return pl.pallas_call(
         _term_kernel,
-        in_specs=[vm] * 2,
-        out_specs=vm,
-        out_shape=jax.ShapeDtypeStruct((128, 64, 256), F32),
+        in_specs=[vm] * 4,
+        out_specs=[vm] * 2,
+        out_shape=[jax.ShapeDtypeStruct((128, 64, 256), F32), jax.ShapeDtypeStruct((64, 2048), BF16)],
         compiler_params=pltpu.CompilerParams(vmem_limit_bytes=VMEM),
         cost_estimate=pl.CostEstimate(flops=400_000_000, bytes_accessed=12_000_000, transcendentals=0),
         name="term",
-    )(u, sf)
+    )(u, sf, hg, both)
 
 
 def _fine_kernel(
@@ -547,11 +552,11 @@
     mixed, p, s = mix_call(place, got, lift, weight)
     mine, other = to_all(mixed)
     su, sut, fine = upstream_call(held, u)
-    keep, send, hl = hidden_call(
+    keep, send, hg, both = hidden_call(
         place, mine, other, ps, pst, su, sut, lift, skip, down.T, fine, syn, ana, to_grid, to_modes
     )
     far = other_core(send)
-    term = term_call(u, skip_fine)
+    term, hl = term_call(u, skip_fine, hg, both)
     keep, term = lax.optimization_barrier((keep, term))
     summed = (keep + far).reshape(320, 4, 128)
     got = lax.all_to_all(summed, SAME_CORE, 0, 0, tiled=True).reshape(64, 5, 4, 128)

time: 105 us -> 105 us (level)
  no operation moved by 1% of the time
where the time goes in v3:
time: 105 us
  blocking collectives  74.8 us (71%)
  Pallas kernels  21.9 us (21%)
  starting transfers between devices  5.98 us (6%)
    all_to_all x2, blocking collectives, to_all(): mine = lax.all_to_all(copies, SAME_CORE, 0, 0, tiled=True)  33.9 us
    all_to_all x1, blocking collectives, body(): got = lax.all_to_all(partial.reshape(128, 4, 128), ALL, 0, 0, tiled=True)  22.6 us
    all_to_all x1, blocking collectives, body(): lax.all_to_all(summed, SAME_CORE, 0, 0, tiled=True).reshape(64, 5, 4, 128)  18.3 us
    ppermute x3, starting transfers between devices, other_core(): return lax.ppermute(a, 'core', [(0, 1), (1, 0)])  5.98 us
    pallas_call x1, Pallas kernels, hidden_call(): pl.pallas_call(_hidden_kernel, in_specs=[pl.BlockSpec(memory_space=pltpu....  5.13 us
    pallas_call x1, Pallas kernels, fine_call(): pl.pallas_call(_fine_kernel, in_specs=[pl.BlockSpec(memory_space=pltpu.SM...  4.76 us
    pallas_call x1, Pallas kernels, pool_call(): pl.pallas_call(_pool_kernel, in_specs=[pl.BlockSpec(memory_space=pltpu.SM...  4.61 us
  transfers between devices with their start and end apart: 3, of which 2 were waited for; matrix products, arithmetic and copies ran while one was open for 0% of the time, Pallas kernels for 5%

profile of v3, /device:TPU:1, one launch (start us, length us, event | category | flops | bytes accessed | tf_op | source)
XLA Modules:
  0.0 104.5 jit_solution(11091362081094540467)
XLA Ops:
  0.6 0.1 pad_add_fusion.place_ref
  0.7 0.0 copy-start.1
  0.7 0.0 copy-start.3
  0.7 0.0 copy-start
  0.7 4.6 %pool.1 = (f32[32,4,4,128]{3,2,1,0:T(4,128)S(1)}, bf16[32,64,128]{2,1,0:T(8,128)(2,1)S(1)}, bf16[64,2048]{1,0:T(8,128)(2,1)S(1)}, bf16[64,64]{1,0:T(8,128)(2,1)S...) custom-call(s32[3]{0:T(128)S(1)} %pad_add_fusion.place_ref, ...), custom_call_target="tpu_custom_call" | custom-call | tf_op jit(solution)/shard_map/pool/pallas_call | solution.py:167
  5.3 22.6 %all_to_all.20.got_ref = f32[128,4,128]{2,1,0:T(4,128)S(1)} all-to-all(f32[128,4,128]{2,1,0:T(4,128)S(1)} %bitcast.21), channel_id=1, replica_groups=mesh['z'=4,'xl'=2,'core'=2,'y'=4,'xh'=2] {'z','xl','core','y','xh'}, dimensions={0} | all-to-all | bytes 524288 | tf_op jit(solution)/shard_map/all_to_all | solution.py:551
  27.9 0.0 copy-done.1
  27.9 0.0 copy-done.3
  27.9 1.1 %mix.1 = (f32[64,8,256]{2,1,0:T(8,128)S(1)}, f32[8,64]{1,0:T(8,128)S(1)}, f32[8,256]{1,0:T(8,128)S(1)}) custom-call(s32[3]{0:T(128)S(1)} %pad_add_fusion.place_ref, f32[128,4,128]{2,1,0:T(4,128)S(1)} %all_to_all.20.got_ref, bf16[64,256]{1,0:T(8,128)(2,1)S(1)} %copy-done.3, bf16[2,4,256,256]{3,2,1,0:T(8,128)(2,1)S(1)} %copy-done.1), custom_call_target="tpu_custom_call" | custom-call | tf_op jit(solution)/shard_map/mix/pallas_call | solution.py:247
  29.1 15.9 %all_to_all.21 = f32[64,8,256]{2,1,0:T(8,128)S(1)} all-to-all(f32[64,8,256]{2,1,0:T(8,128)S(1)} %get-tuple-element.40), channel_id=1, replica_groups=mesh['z'=4,'xl'=2,'core'=2,'y'=4,'xh'=2] {'y','xh','z','xl'}, dimensions={0} | all-to-all | bytes 1048576 | tf_op jit(solution)/shard_map/all_to_all | solution.py:537
  45.0 2.5 %collective-permute-start = (f32[2,4,8,8,256]{4,3,2,1,0:T(8,128)S(1)}, f32[2,4,8,8,256]{4,3,2,1,0:T(8,128)S(1)}, u32[]{:S(2)}, u32[]{:S(2)}) collective-permute-start(f32[2,4,8,8,256]{4,3,2,1,0:T(8,128)S(1)} %bitcast.19), channel_id=1, source_target_pairs={{0,8},{8,0},{1,9},{9,1},{2,10},{10,2},{3,11},{11,3},{4,12},{12,4},... | collective-permute-start | bytes 1572872 | tf_op jit(solution)/shard_map/ppermute | solution.py:533
  47.5 0.0 copy-done
  47.5 0.0 copy-start.2
  47.5 0.0 copy-start.4
  47.5 0.0 copy-start.5
  47.5 1.9 %upstream.1 = (bf16[32,64,64]{2,1,0:T(8,128)(2,1)S(1)}, bf16[64,2048]{1,0:T(8,128)(2,1)S(1)}, f32[64,64]{1,0:T(8,128)S(1)}) custom-call(bf16[128,64,256]{2,1,0:T(8,128)(2,1)S(1)} %get-tuple-element.43.x_ref, bf16[128,64,256]{2,1,0:T(8,128)(2,1)S(1)} %bitcast.13), custom_call_target="tpu_custom_call" | custom-call | tf_op jit(solution)/shard_map/upstream/pallas_call | solution.py:210
  49.4 0.0 collective-permute-done.other_ref
  49.4 0.0 copy-done.2
  49.4 0.0 copy-done.4
  49.4 5.1 %hidden.1 = (f32[2,4,8,5,4,128]{5,4,3,2,1,0:T(4,128)S(1)}, f32[2,4,8,5,4,128]{5,4,3,2,1,0:T(4,128)S(1)}, bf16[2048,256]{1,0:T(8,128)(2,1)S(1)}, bf16[64,256]{1,0:T(8,128)(2,1)S(1)}) custom-call(s32[3]{0:T(128)S(1)} %pad_add_fusion.place_ref, f32[2,4,8,8,256]{4,3,2,1,0:T(8,128)S(1)} %bitcast.20, f32[2,4,8,8,256]{4,3,2,1,0:T(8,128)S(1)} %collective-permute-done.other_ref, ...), custom_call_target="tpu_custom_call" | custom-call | tf_op jit(solution)/shard_map/hidden/pallas_call | solution.py:326
  54.6 0.1 collective-permute-start.1
  54.7 0.0 copy-done.5
  54.7 1.6 %term.1 = (f32[128,64,256]{2,1,0:T(8,128)S(1)}, bf16[64,2048]{1,0:T(8,128)(2,1)S(1)}) custom-call(bf16[128,64,256]{2,1,0:T(8,128)(2,1)S(1)} %bitcast.14, bf16[64,64]{1,0:T(8,128)(2,1)S(1)} %copy-done.5, bf16[2048,256]{1,0:T(8,128)(2,1)S(1)} %get-tuple-element.52.hg_ref, bf16[64,256]{1,0:T(8,128)(2,1)S(1)} %get-tuple-element.53.both_ref), custom_call_target="tpu_custom_call" | custom-call | flops 400000000 | bytes 12000000 | tf_op jit(solution)/shard_map/term/pallas_call | solution.py:444
  56.3 0.5 collective-permute-done.1
  56.8 0.2 add.15
  56.9 18.3 %all_to_all.22 = f32[320,4,128]{2,1,0:T(4,128)S(1)} all-to-all(f32[320,4,128]{2,1,0:T(4,128)S(1)} %bitcast.24), channel_id=1, replica_groups=mesh['z'=4,'xl'=2,'core'=2,'y'=4,'xh'=2] {'y','xh','z','xl'}, dimensions={0} | all-to-all | bytes 1310720 | tf_op jit(solution)/shard_map/all_to_all | solution.py:562
  75.2 1.1 %adjoint.1 = (f32[8,256]{1,0:T(8,128)S(1)}, f32[64,8,384]{2,1,0:T(8,128)S(1)}) custom-call(s32[3]{0:T(128)S(1)} %pad_add_fusion.place_ref, f32[64,5,4,128]{3,2,1,0:T(4,128)S(1)} %bitcast.18, f32[8,64]{1,0:T(8,128)S(1)} %get-tuple-element.59.p_ref, bf16[2,4,256,256]{3,2,1,0:T(8,128)(2,1)S(1)} %copy-done.1), custom_call_target="tpu_custom_call" | custom-call | tf_op jit(solution)/shard_map/adjoint/pallas_call | solution.py:373
  76.2 18.0 %all_to_all.23 = f32[64,8,384]{2,1,0:T(8,128)S(1)} all-to-all(f32[64,8,384]{2,1,0:T(8,128)S(1)} %get-tuple-element.60), channel_id=1, replica_groups=mesh['z'=4,'xl'=2,'core'=2,'y'=4,'xh'=2] {'y','xh','z','xl'}, dimensions={0} | all-to-all | bytes 1572864 | tf_op jit(solution)/shard_map/all_to_all | solution.py:537
  94.3 3.4 %collective-permute-start.2 = (f32[2,4,8,8,384]{4,3,2,1,0:T(8,128)S(1)}, f32[2,4,8,8,384]{4,3,2,1,0:T(8,128)S(1)}, u32[]{:S(2)}, u32[]{:S(2)}) collective-permute-start(f32[2,4,8,8,384]{4,3,2,1,0:T(8,128)S(1)} %bitcast.15), channel_id=1, source_target_pairs={{0,8},{8,0},{1,9},{9,1},{2,10},{10,2},{3,11},{11,3},{4,12},{12,4},... | collective-permute-start | bytes 2359304 | tf_op jit(solution)/shard_map/ppermute | solution.py:533
  97.7 1.7 %outer.1 = (f32[2,4,256,256]{3,2,1,0:T(8,128)}, f32[512,64]{1,0:T(8,128)S(1)}, f32[64,256]{1,0:T(8,128)S(1)}) custom-call(f32[8,256]{1,0:T(8,128)S(1)} %get-tuple-element.61.s_ref, f32[8,256]{1,0:T(8,128)S(1)} %get-tuple-element.62.pulled_ref, f32[2,4,8,8,384]{4,3,2,1,0:T(8,128)S(1)} %bitcast.16, bf16[64,256]{1,0:T(8,128)(2,1)S(1)} %copy-done.3), custom_call_target="tpu_custom_call" | custom-call | flops 2000000 | bytes 2200000 | tf_op jit(solution)/shard_map/outer/pallas_call | solution.py:413
  99.4 0.2 collective-permute-done.2.other_ref
  99.6 4.8 %fine.1 = (bf16[128,64,256]{2,1,0:T(8,128)(2,1)}, f32[64,256]{1,0:T(8,128)}, f32[256,256]{1,0:T(8,128)}, f32[64,256]{1,0:T(8,128)}, f32[64,64]{1,0:T(8,128)}) custom-call(s32[3]{0:T(128)S(1)} %pad_add_fusion.place_ref, f32[128,64,256]{2,1,0:T(8,128)S(1)} %get-tuple-element.55.term_ref, bf16[64,2048]{1,0:T(8,128)(2,1)S(1)} %get-tuple-element.56.hl_ref, ...), custom_call_target="tpu_custom_call" | custom-call | tf_op jit(solution)/shard_map/fine/pallas_call | solution.py:511
Async XLA Ops:
  0.7 27.2 %copy-start.1 = (bf16[2,4,256,256]{3,2,1,0:T(8,128)(2,1)S(1)}, bf16[2,4,256,256]{3,2,1,0:T(8,128)(2,1)}, u32[]{:S(2)}) copy-start(bf16[2,4,256,256]{3,2,1,0:T(8,128)(2,1)} %w_ref.3) | copy-start | bytes 3145732
  0.7 27.2 %copy-start.3 = (bf16[64,256]{1,0:T(8,128)(2,1)S(1)}, bf16[64,256]{1,0:T(8,128)(2,1)}, u32[]{:S(2)}) copy-start(bf16[64,256]{1,0:T(8,128)(2,1)} %lift_ref.7) | copy-start | bytes 98308
  0.7 46.7 %copy-start = (bf16[128,256,64]{1,2,0:T(8,128)(2,1)S(1)}, bf16[128,256,64]{1,2,0:T(8,128)(2,1)}, u32[]{:S(2)}) copy-start(bf16[128,256,64]{1,2,0:T(8,128)(2,1)} %param.14) | copy-start | bytes 12582916
  45.0 4.4 %collective-permute-start = (f32[2,4,8,8,256]{4,3,2,1,0:T(8,128)S(1)}, f32[2,4,8,8,256]{4,3,2,1,0:T(8,128)S(1)}, u32[]{:S(2)}, u32[]{:S(2)}) collective-permute-start(f32[2,4,8,8,256]{4,3,2,1,0:T(8,128)S(1)} %bitcast.19), channel_id=1, source_target_pairs={{0,8},{8,0},{1,9},{9,1},{2,10},{10,2},{3,11},{11,3},{4,12},{12,4},... | collective-permute-start | bytes 1572872 | tf_op jit(solution)/shard_map/ppermute | solution.py:533
  47.5 2.0 %copy-start.2 = (bf16[256,256]{1,0:T(8,128)(2,1)S(1)}, bf16[256,256]{1,0:T(8,128)(2,1)}, u32[]{:S(2)}) copy-start(bf16[256,256]{1,0:T(8,128)(2,1)} %skip_ref.3) | copy-start | bytes 393220
  47.5 2.0 %copy-start.4 = (bf16[256,64]{0,1:T(8,128)(2,1)S(1)}, bf16[256,64]{0,1:T(8,128)(2,1)}, u32[]{:S(2)}) copy-start(bf16[256,64]{0,1:T(8,128)(2,1)} %param.18) | copy-start | bytes 98308
  47.5 7.2 %copy-start.5 = (bf16[64,64]{1,0:T(8,128)(2,1)S(1)}, bf16[64,64]{1,0:T(8,128)(2,1)}, u32[]{:S(2)}) copy-start(bf16[64,64]{1,0:T(8,128)(2,1)} %sf_ref.1) | copy-start | bytes 24580
  54.6 2.2 %collective-permute-start.1 = (f32[2,4,8,5,4,128]{5,4,3,2,1,0:T(4,128)S(1)}, f32[2,4,8,5,4,128]{5,4,3,2,1,0:T(4,128)S(1)}, u32[]{:S(2)}, u32[]{:S(2)}) collective-permute-start(f32[2,4,8,5,4,128]{5,4,3,2,1,0:T(4,128)S(1)} %get-tuple-element.58), channel_id=1, source_target_pairs={{0,8},{8,0},{1,9},{9,1},{2,10},{10,2},{3,11},{11,3},{4,12},{12,4},... | collective-permute-start | bytes 1966088 | tf_op jit(solution)/shard_map/ppermute | solution.py:533
  94.3 5.3 %collective-permute-start.2 = (f32[2,4,8,8,384]{4,3,2,1,0:T(8,128)S(1)}, f32[2,4,8,8,384]{4,3,2,1,0:T(8,128)S(1)}, u32[]{:S(2)}, u32[]{:S(2)}) collective-permute-start(f32[2,4,8,8,384]{4,3,2,1,0:T(8,128)S(1)} %bitcast.15), channel_id=1, source_target_pairs={{0,8},{8,0},{1,9},{9,1},{2,10},{10,2},{3,11},{11,3},{4,12},{12,4},... | collective-permute-start | bytes 2359304 | tf_op jit(solution)/shard_map/ppermute | solution.py:533

commit v4 on v3

--- a/solution.py
+++ b/solution.py
@@ -391,7 +391,15 @@
     return narrow, both[:64] + both[64:] + _dot(p_high, low)
 
 
-def _outer_kernel(s_ref, pulled_ref, mine_ref, lift_ref, grad_any, narrow_ref, sum_ref, grad_ref, sem):
+def _turn_class(table_ref, apart, narrow, g):
+    table_high = table_ref[:, 128 * apart : 128 * apart + 128]
+    table_low = table_ref[:, 256 + 128 * apart : 384 + 128 * apart]
+    high, low = _halves(narrow.reshape(2, 4, 8, 8, 64)[:, g].reshape(128, 64))
+    turned = _dot(jnp.concatenate([table_high, table_low], 1), jnp.concatenate([high, high], 0))
+    return (turned + _dot(table_high, low)).reshape(32, 8, 64)
+
+
+def _outer_kernel(s_ref, pulled_ref, mine_ref, lift_ref, syn_ref, grad_any, near_ref, sum_ref, grad_ref, sem):
     s = s_ref[...].T
     pulled = pulled_ref[...]
     copies = []
@@ -403,27 +411,29 @@
         for part in range(2):
             copies.append(pltpu.make_async_copy(grad_ref.at[part, t], grad_any.at[part, t], sem.at[part, t]))
             copies[-1].start()
-    narrow_ref[...], sum_ref[...] = _gathered(mine_ref, lift_ref[...])
+    narrow, sum_ref[...] = _gathered(mine_ref, lift_ref[...])
+    for g in range(4):
+        near_ref[:, g * 8 : (g + 1) * 8, :] = _turn_class(syn_ref, 0, narrow, g)
     for copy in copies:
         copy.wait()
 
 
-def outer_call(s, pulled, mine, lift):
+def outer_call(s, pulled, mine, lift, syn):
     vm = pl.BlockSpec(memory_space=pltpu.VMEM)
     return pl.pallas_call(
         _outer_kernel,
-        in_specs=[vm] * 4,
+        in_specs=[vm] * 5,
         out_specs=[pl.BlockSpec(memory_space=pl.ANY), vm, vm],
         out_shape=[
             jax.ShapeDtypeStruct((2, 4, 256, 256), F32),
-            jax.ShapeDtypeStruct((512, 64), F32),
+            jax.ShapeDtypeStruct((32, 32, 64), F32),
             jax.ShapeDtypeStruct((64, 256), F32),
         ],
         scratch_shapes=[pltpu.VMEM((2, 4, 256, 256), F32), pltpu.SemaphoreType.DMA((2, 4))],
         compiler_params=pltpu.CompilerParams(vmem_limit_bytes=VMEM),
         cost_estimate=pl.CostEstimate(flops=2_000_000, bytes_accessed=2_200_000, transcendentals=0),
         name="outer",
-    )(s, pulled, mine, lift)
+    )(s, pulled, mine, lift, syn)
 
 
 def _term_kernel(u_ref, sf_ref, hg_ref, both_ref, out_ref, hl_ref):
@@ -453,15 +463,14 @@
 
 
 def _fine_kernel(
-    place_ref, term_ref, hl_ref, mine_ref, narrow_ref, sum_ref, other_ref, lift_ref, skip_ref, syn_ref, wide_ref,
+    place_ref, term_ref, hl_ref, mine_ref, near_ref, sum_ref, other_ref, lift_ref, skip_ref, syn_ref, wide_ref,
     out_any, lift_out, skip_out, down_out, fine_out, t_ref, out_ref, sem,
 ):
     lift = lift_ref[...]
     far_narrow, far_sum = _gathered(other_ref, lift)
-    narrow = [a.reshape(2, 4, 8, 8, 64) for a in (narrow_ref[...], far_narrow)]
     for g in range(4):
-        modes = jnp.concatenate([half[:, g].reshape(128, 64) for half in narrow], 0)
-        t_ref[:, g * 8 : (g + 1) * 8, :] = _turn(syn_ref[...], modes).reshape(32, 8, 64)
+        own = slice(g * 8, (g + 1) * 8)
+        t_ref[:, own, :] = near_ref[:, own, :] + _turn_class(syn_ref, 1, far_narrow, g)
 
     def chunk_copy(i):
         at = pl.ds(i * 16, 16)
@@ -562,9 +571,9 @@
     got = lax.all_to_all(summed, SAME_CORE, 0, 0, tiled=True).reshape(64, 5, 4, 128)
     pulled, block = adjoint_call(place, got, p, weight)
     mine, other = to_all(block)
-    grad_spectral, narrow, lift_sum = outer_call(s, pulled, mine, lift)
+    grad_spectral, near, lift_sum = outer_call(s, pulled, mine, lift, syn)
     grad_input, g_lift, g_skip, g_down, g_fine = fine_call(
-        place, term, hl, mine, narrow, lift_sum, other, lift, skip, syn, to_fine
+        place, term, hl, mine, near, lift_sum, other, lift, skip, syn, to_fine
     )
     return grad_input.transpose(0, 2, 1), grad_spectral, g_lift, g_skip, g_down.T, g_fine
 

time: 105 us -> 104 us (level)
  no operation moved by 1% of the time
where the time goes in v4:
time: 104 us
  blocking collectives  74.8 us (72%)
  Pallas kernels  21.6 us (21%)
  starting transfers between devices  5.98 us (6%)
    all_to_all x2, blocking collectives, to_all(): mine = lax.all_to_all(copies, SAME_CORE, 0, 0, tiled=True)  33.9 us
    all_to_all x1, blocking collectives, body(): got = lax.all_to_all(partial.reshape(128, 4, 128), ALL, 0, 0, tiled=True)  22.6 us
    all_to_all x1, blocking collectives, body(): lax.all_to_all(summed, SAME_CORE, 0, 0, tiled=True).reshape(64, 5, 4, 128)  18.3 us
    ppermute x3, starting transfers between devices, other_core(): return lax.ppermute(a, 'core', [(0, 1), (1, 0)])  5.98 us
    pallas_call x1, Pallas kernels, hidden_call(): pl.pallas_call(_hidden_kernel, in_specs=[pl.BlockSpec(memory_space=pltpu....  5.1 us
    pallas_call x1, Pallas kernels, pool_call(): pl.pallas_call(_pool_kernel, in_specs=[pl.BlockSpec(memory_space=pltpu.SM...  4.61 us
    pallas_call x1, Pallas kernels, fine_call(): pl.pallas_call(_fine_kernel, in_specs=[pl.BlockSpec(memory_space=pltpu.SM...  4.53 us
  transfers between devices with their start and end apart: 3, of which 2 were waited for; matrix products, arithmetic and copies ran while one was open for 0% of the time, Pallas kernels for 5%

profile of v4, /device:TPU:1, one launch (start us, length us, event | category | flops | bytes accessed | tf_op | source)
XLA Modules:
  0.0 104.3 jit_solution(18437333630067124666)
XLA Ops:
  0.6 0.1 pad_add_fusion.place_ref
  0.7 0.0 copy-start.1
  0.7 0.0 copy-start.3
  0.7 0.0 copy-start
  0.7 4.6 %pool.1 = (f32[32,4,4,128]{3,2,1,0:T(4,128)S(1)}, bf16[32,64,128]{2,1,0:T(8,128)(2,1)S(1)}, bf16[64,2048]{1,0:T(8,128)(2,1)S(1)}, bf16[64,64]{1,0:T(8,128)(2,1)S...) custom-call(s32[3]{0:T(128)S(1)} %pad_add_fusion.place_ref, ...), custom_call_target="tpu_custom_call" | custom-call | tf_op jit(solution)/shard_map/pool/pallas_call | solution.py:167
  5.3 22.6 %all_to_all.20.got_ref = f32[128,4,128]{2,1,0:T(4,128)S(1)} all-to-all(f32[128,4,128]{2,1,0:T(4,128)S(1)} %bitcast.21), channel_id=1, replica_groups=mesh['z'=4,'xl'=2,'core'=2,'y'=4,'xh'=2] {'z','xl','core','y','xh'}, dimensions={0} | all-to-all | bytes 524288 | tf_op jit(solution)/shard_map/all_to_all | solution.py:560
  27.9 0.0 copy-done.1
  27.9 0.0 copy-done.3
  27.9 1.1 %mix.1 = (f32[64,8,256]{2,1,0:T(8,128)S(1)}, f32[8,64]{1,0:T(8,128)S(1)}, f32[8,256]{1,0:T(8,128)S(1)}) custom-call(s32[3]{0:T(128)S(1)} %pad_add_fusion.place_ref, f32[128,4,128]{2,1,0:T(4,128)S(1)} %all_to_all.20.got_ref, bf16[64,256]{1,0:T(8,128)(2,1)S(1)} %copy-done.3, bf16[2,4,256,256]{3,2,1,0:T(8,128)(2,1)S(1)} %copy-done.1), custom_call_target="tpu_custom_call" | custom-call | tf_op jit(solution)/shard_map/mix/pallas_call | solution.py:247
  29.1 15.9 %all_to_all.21 = f32[64,8,256]{2,1,0:T(8,128)S(1)} all-to-all(f32[64,8,256]{2,1,0:T(8,128)S(1)} %get-tuple-element.40), channel_id=1, replica_groups=mesh['z'=4,'xl'=2,'core'=2,'y'=4,'xh'=2] {'y','xh','z','xl'}, dimensions={0} | all-to-all | bytes 1048576 | tf_op jit(solution)/shard_map/all_to_all | solution.py:546
  45.0 2.5 %collective-permute-start = (f32[2,4,8,8,256]{4,3,2,1,0:T(8,128)S(1)}, f32[2,4,8,8,256]{4,3,2,1,0:T(8,128)S(1)}, u32[]{:S(2)}, u32[]{:S(2)}) collective-permute-start(f32[2,4,8,8,256]{4,3,2,1,0:T(8,128)S(1)} %bitcast.19), channel_id=1, source_target_pairs={{0,8},{8,0},{1,9},{9,1},{2,10},{10,2},{3,11},{11,3},{4,12},{12,4},... | collective-permute-start | bytes 1572872 | tf_op jit(solution)/shard_map/ppermute | solution.py:542
  47.5 0.0 copy-done
  47.5 0.0 copy-start.2
  47.5 0.0 copy-start.4
  47.5 0.0 copy-start.5
  47.5 1.9 %upstream.1 = (bf16[32,64,64]{2,1,0:T(8,128)(2,1)S(1)}, bf16[64,2048]{1,0:T(8,128)(2,1)S(1)}, f32[64,64]{1,0:T(8,128)S(1)}) custom-call(bf16[128,64,256]{2,1,0:T(8,128)(2,1)S(1)} %get-tuple-element.43.x_ref, bf16[128,64,256]{2,1,0:T(8,128)(2,1)S(1)} %bitcast.13), custom_call_target="tpu_custom_call" | custom-call | tf_op jit(solution)/shard_map/upstream/pallas_call | solution.py:210
  49.4 0.0 collective-permute-done.other_ref
  49.4 0.0 copy-done.2
  49.4 0.0 copy-done.4
  49.4 5.1 %hidden.1 = (f32[2,4,8,5,4,128]{5,4,3,2,1,0:T(4,128)S(1)}, f32[2,4,8,5,4,128]{5,4,3,2,1,0:T(4,128)S(1)}, bf16[2048,256]{1,0:T(8,128)(2,1)S(1)}, bf16[64,256]{1,0:T(8,128)(2,1)S(1)}) custom-call(s32[3]{0:T(128)S(1)} %pad_add_fusion.place_ref, f32[2,4,8,8,256]{4,3,2,1,0:T(8,128)S(1)} %bitcast.20, f32[2,4,8,8,256]{4,3,2,1,0:T(8,128)S(1)} %collective-permute-done.other_ref, ...), custom_call_target="tpu_custom_call" | custom-call | tf_op jit(solution)/shard_map/hidden/pallas_call | solution.py:326
  54.6 0.1 collective-permute-start.1
  54.7 0.0 copy-done.5
  54.7 1.6 %term.1 = (f32[128,64,256]{2,1,0:T(8,128)S(1)}, bf16[64,2048]{1,0:T(8,128)(2,1)S(1)}) custom-call(bf16[128,64,256]{2,1,0:T(8,128)(2,1)S(1)} %bitcast.14, bf16[64,64]{1,0:T(8,128)(2,1)S(1)} %copy-done.5, bf16[2048,256]{1,0:T(8,128)(2,1)S(1)} %get-tuple-element.52.hg_ref, bf16[64,256]{1,0:T(8,128)(2,1)S(1)} %get-tuple-element.53.both_ref), custom_call_target="tpu_custom_call" | custom-call | flops 400000000 | bytes 12000000 | tf_op jit(solution)/shard_map/term/pallas_call | solution.py:454
  56.2 0.5 collective-permute-done.1
  56.7 0.2 add.15
  56.9 18.3 %all_to_all.22 = f32[320,4,128]{2,1,0:T(4,128)S(1)} all-to-all(f32[320,4,128]{2,1,0:T(4,128)S(1)} %bitcast.24), channel_id=1, replica_groups=mesh['z'=4,'xl'=2,'core'=2,'y'=4,'xh'=2] {'y','xh','z','xl'}, dimensions={0} | all-to-all | bytes 1310720 | tf_op jit(solution)/shard_map/all_to_all | solution.py:571
  75.2 1.1 %adjoint.1 = (f32[8,256]{1,0:T(8,128)S(1)}, f32[64,8,384]{2,1,0:T(8,128)S(1)}) custom-call(s32[3]{0:T(128)S(1)} %pad_add_fusion.place_ref, f32[64,5,4,128]{3,2,1,0:T(4,128)S(1)} %bitcast.18, f32[8,64]{1,0:T(8,128)S(1)} %get-tuple-element.59.p_ref, bf16[2,4,256,256]{3,2,1,0:T(8,128)(2,1)S(1)} %copy-done.1), custom_call_target="tpu_custom_call" | custom-call | tf_op jit(solution)/shard_map/adjoint/pallas_call | solution.py:373
  76.2 18.0 %all_to_all.23 = f32[64,8,384]{2,1,0:T(8,128)S(1)} all-to-all(f32[64,8,384]{2,1,0:T(8,128)S(1)} %get-tuple-element.60), channel_id=1, replica_groups=mesh['z'=4,'xl'=2,'core'=2,'y'=4,'xh'=2] {'y','xh','z','xl'}, dimensions={0} | all-to-all | bytes 1572864 | tf_op jit(solution)/shard_map/all_to_all | solution.py:546
  94.3 3.4 %collective-permute-start.2 = (f32[2,4,8,8,384]{4,3,2,1,0:T(8,128)S(1)}, f32[2,4,8,8,384]{4,3,2,1,0:T(8,128)S(1)}, u32[]{:S(2)}, u32[]{:S(2)}) collective-permute-start(f32[2,4,8,8,384]{4,3,2,1,0:T(8,128)S(1)} %bitcast.15), channel_id=1, source_target_pairs={{0,8},{8,0},{1,9},{9,1},{2,10},{10,2},{3,11},{11,3},{4,12},{12,4},... | collective-permute-start | bytes 2359304 | tf_op jit(solution)/shard_map/ppermute | solution.py:542
  97.7 1.7 %outer.1 = (f32[2,4,256,256]{3,2,1,0:T(8,128)}, f32[32,32,64]{2,1,0:T(8,128)S(1)}, f32[64,256]{1,0:T(8,128)S(1)}) custom-call(f32[8,256]{1,0:T(8,128)S(1)} %get-tuple-element.61.s_ref, f32[8,256]{1,0:T(8,128)S(1)} %get-tuple-element.62.pulled_ref, f32[2,4,8,8,384]{4,3,2,1,0:T(8,128)S(1)} %bitcast.16, bf16[64,256]{1,0:T(8,128)(2,1)S(1)} %copy-done.3, ...), custom_call_target="tpu_custom_call" | custom-call | flops 2000000 | bytes 2200000 | tf_op jit(solution)/shard_map/outer/pallas_call | solution.py:423
  99.3 0.2 collective-permute-done.2.other_ref
  99.6 4.5 %fine.1 = (bf16[128,64,256]{2,1,0:T(8,128)(2,1)}, f32[64,256]{1,0:T(8,128)}, f32[256,256]{1,0:T(8,128)}, f32[64,256]{1,0:T(8,128)}, f32[64,64]{1,0:T(8,128)}) custom-call(s32[3]{0:T(128)S(1)} %pad_add_fusion.place_ref, f32[128,64,256]{2,1,0:T(8,128)S(1)} %get-tuple-element.55.term_ref, bf16[64,2048]{1,0:T(8,128)(2,1)S(1)} %get-tuple-element.56.hl_ref, ...), custom_call_target="tpu_custom_call" | custom-call | tf_op jit(solution)/shard_map/fine/pallas_call | solution.py:520
Async XLA Ops:
  0.7 27.2 %copy-start.1 = (bf16[2,4,256,256]{3,2,1,0:T(8,128)(2,1)S(1)}, bf16[2,4,256,256]{3,2,1,0:T(8,128)(2,1)}, u32[]{:S(2)}) copy-start(bf16[2,4,256,256]{3,2,1,0:T(8,128)(2,1)} %w_ref.3) | copy-start | bytes 3145732
  0.7 27.2 %copy-start.3 = (bf16[64,256]{1,0:T(8,128)(2,1)S(1)}, bf16[64,256]{1,0:T(8,128)(2,1)}, u32[]{:S(2)}) copy-start(bf16[64,256]{1,0:T(8,128)(2,1)} %lift_ref.7) | copy-start | bytes 98308
  0.7 46.7 %copy-start = (bf16[128,256,64]{1,2,0:T(8,128)(2,1)S(1)}, bf16[128,256,64]{1,2,0:T(8,128)(2,1)}, u32[]{:S(2)}) copy-start(bf16[128,256,64]{1,2,0:T(8,128)(2,1)} %param.14) | copy-start | bytes 12582916
  45.0 4.4 %collective-permute-start = (f32[2,4,8,8,256]{4,3,2,1,0:T(8,128)S(1)}, f32[2,4,8,8,256]{4,3,2,1,0:T(8,128)S(1)}, u32[]{:S(2)}, u32[]{:S(2)}) collective-permute-start(f32[2,4,8,8,256]{4,3,2,1,0:T(8,128)S(1)} %bitcast.19), channel_id=1, source_target_pairs={{0,8},{8,0},{1,9},{9,1},{2,10},{10,2},{3,11},{11,3},{4,12},{12,4},... | collective-permute-start | bytes 1572872 | tf_op jit(solution)/shard_map/ppermute | solution.py:542
  47.5 2.0 %copy-start.2 = (bf16[256,256]{1,0:T(8,128)(2,1)S(1)}, bf16[256,256]{1,0:T(8,128)(2,1)}, u32[]{:S(2)}) copy-start(bf16[256,256]{1,0:T(8,128)(2,1)} %skip_ref.3) | copy-start | bytes 393220
  47.5 2.0 %copy-start.4 = (bf16[256,64]{0,1:T(8,128)(2,1)S(1)}, bf16[256,64]{0,1:T(8,128)(2,1)}, u32[]{:S(2)}) copy-start(bf16[256,64]{0,1:T(8,128)(2,1)} %param.18) | copy-start | bytes 98308
  47.5 7.2 %copy-start.5 = (bf16[64,64]{1,0:T(8,128)(2,1)S(1)}, bf16[64,64]{1,0:T(8,128)(2,1)}, u32[]{:S(2)}) copy-start(bf16[64,64]{1,0:T(8,128)(2,1)} %sf_ref.1) | copy-start | bytes 24580
  54.6 2.2 %collective-permute-start.1 = (f32[2,4,8,5,4,128]{5,4,3,2,1,0:T(4,128)S(1)}, f32[2,4,8,5,4,128]{5,4,3,2,1,0:T(4,128)S(1)}, u32[]{:S(2)}, u32[]{:S(2)}) collective-permute-start(f32[2,4,8,5,4,128]{5,4,3,2,1,0:T(4,128)S(1)} %get-tuple-element.58), channel_id=1, source_target_pairs={{0,8},{8,0},{1,9},{9,1},{2,10},{10,2},{3,11},{11,3},{4,12},{12,4},... | collective-permute-start | bytes 1966088 | tf_op jit(solution)/shard_map/ppermute | solution.py:542
  94.3 5.3 %collective-permute-start.2 = (f32[2,4,8,8,384]{4,3,2,1,0:T(8,128)S(1)}, f32[2,4,8,8,384]{4,3,2,1,0:T(8,128)S(1)}, u32[]{:S(2)}, u32[]{:S(2)}) collective-permute-start(f32[2,4,8,8,384]{4,3,2,1,0:T(8,128)S(1)} %bitcast.15), channel_id=1, source_target_pairs={{0,8},{8,0},{1,9},{9,1},{2,10},{10,2},{3,11},{11,3},{4,12},{12,4},... | collective-permute-start | bytes 2359304 | tf_op jit(solution)/shard_map/ppermute | solution.py:542
